TPU v7x, 256 devices: a whole 4x4x8 slice. The times are simulated.
256 devices in a mesh: inst: 16 (over y, x), cell: 16 (over z, core).
Axes of the slice: x: 4, y: 4, z: 8, core: 2. Of those that a mesh axis runs over, the one named last changes fastest.
Arguments:
- state: float32 [16, 4, 512, 2048], P('inst', None, None, 'cell'), may hold values from -1.2 to 3, as said below
- src_inst: int32 [4, 16, 2048], P(None, 'inst', 'cell'), may hold values from 0 to 15, as said below
- src_face: int32 [4, 16, 2048], P(None, 'inst', 'cell'), may hold values from 0 to 2047, as said below
- weights: float32 [4, 16, 2048], P(None, 'inst', 'cell'), may hold values from 0 to 1, as said below
Outputs:
- residual: float32 [16, 4, 512, 2048], P('inst', None, None, 'cell')
- new_state: float32 [16, 4, 512, 2048], P('inst', None, None, 'cell')
Inputs may be any that keep to these rules, and one draw needn't show every extreme that they name: `src_inst`: entries of a rotor instance (index below 9) name stator instances, entries of a stator instance name rotor instances; entries 0 and 1 of a face name one instance, entries 2 and 3 the next instance of the same row (cyclically within the row). `src_face`: the sliding interface turns each instance by one pitchwise shift s of its own: for face y of instance i, entries 0 and 2 name face (y + s) mod 2048 and entries 1 and 3 name face (y + s + 1) mod 2048. The 4 weights of a face are non-negative and sum to one. `state`: density within 0.8 to 1.25, momenta within -1.2 to 1.2, energy within 2 to 3.
All inputs are finite; a program needn't handle non-finite values.
Results may differ from a plain program's by a relative error of at most 0.0002.
Values sent between devices are 32-bit elements; how exact they have to be, the bound alone decides.
No kernel may reach another device: no remote copies, remote signals or barrier semaphores. Data moves between devices by JAX's collectives and lax.ppermute only.
A program may use at most 128 MiB of HBM per device.

v0:
```python
import jax
import jax.numpy as jnp
import numpy as np
from jax import lax
from jax.sharding import PartitionSpec as P

ROTOR_INST = 9
STATOR_INST = 7
ENTRIES = 4


GAMMA_LESS = 0.4
DAMPING_COEF = 0.05
PSEUDO_STEP = 0.2
OMEGA_ROTOR = 0.8
OMEGA_STATOR = 0.6


def extended(cells, sides, width):
    for axis, dim in sides:
        count = lax.axis_size(axis)
        head = lax.slice_in_dim(cells, 0, width, axis=dim)
        tail = lax.slice_in_dim(cells, cells.shape[dim] - width, cells.shape[dim], axis=dim)
        cells = jnp.concatenate(
            [
                lax.ppermute(tail, axis, [(i, (i + 1) % count) for i in range(count)]),
                cells,
                lax.ppermute(head, axis, [((i + 1) % count, i) for i in range(count)]),
            ],
            axis=dim,
        )
    return cells


def spectral_block(count, omega):
    places = np.arange(count)
    distance = places[:, None] - places[None, :]
    off_diag = distance != 0
    safe = np.where(off_diag, distance, 1)
    values = 0.5 * np.power(-1.0, distance) / np.sin(np.pi * safe / count)
    return np.where(off_diag, values, 0.0) * omega


def spectral_table(rotor_count, stator_count):
    total = rotor_count + stator_count
    matrix = np.zeros((total, total))
    matrix[:rotor_count, :rotor_count] = spectral_block(rotor_count, OMEGA_ROTOR)
    matrix[rotor_count:, rotor_count:] = spectral_block(stator_count, OMEGA_STATOR)
    return jnp.asarray(matrix, jnp.float32)


def flux_along(field, axial):
    density = field[:, 0]
    momentum_x = field[:, 1]
    momentum_y = field[:, 2]
    energy = field[:, 3]
    velocity_x = momentum_x / density
    velocity_y = momentum_y / density
    pressure = GAMMA_LESS * (energy - 0.5 * (momentum_x * velocity_x + momentum_y * velocity_y))
    if axial:
        parts = [
            momentum_x,
            momentum_x * velocity_x + pressure,
            momentum_y * velocity_x,
            (energy + pressure) * velocity_x,
        ]
    else:
        parts = [
            momentum_y,
            momentum_x * velocity_y,
            momentum_y * velocity_y + pressure,
            (energy + pressure) * velocity_y,
        ]
    return jnp.stack(parts, 1)


def on_device(state, src_inst, src_face, weights):
    local_inst = state.shape[0]
    local_width = state.shape[3]
    inst_count = lax.axis_size("inst")
    cell_count = lax.axis_size("cell")
    full_width = local_width * cell_count
    total_inst = local_inst * inst_count
    first_inst = lax.axis_index("inst") * local_inst
    global_inst = first_inst + jnp.arange(local_inst)
    is_rotor = (global_inst < ROTOR_INST)[:, None, None]
    couple = spectral_table(ROTOR_INST, STATOR_INST)
    export = jnp.where(is_rotor, state[:, :, -1, :], state[:, :, 0, :])
    all_rows = lax.all_gather(export[None], ("inst", "cell"), axis=0, tiled=True)
    all_rows = all_rows.reshape(inst_count, cell_count, local_inst, 4, local_width)
    face_table = jnp.transpose(all_rows, (3, 0, 2, 1, 4)).reshape(4, total_inst * full_width)
    mine = lax.dynamic_slice_in_dim(couple, first_inst, local_inst, 0)
    source = jnp.einsum(
        "ij,jcxy->icxy",
        mine,
        lax.all_gather(state, "inst", axis=0, tiled=True),
        precision=lax.Precision.HIGHEST,
    )
    padded_y = extended(state, (("cell", 3),), 1)
    flat_index = src_inst * full_width + src_face
    ghost_row = jnp.zeros((4, local_inst, local_width), jnp.float32)
    for entry in range(ENTRIES):
        ghost_row = ghost_row + weights[entry][None] * jnp.take(
            face_table, flat_index[entry], axis=1
        )
    ghost_row = jnp.transpose(ghost_row, (1, 0, 2))
    left_ghost = jnp.where(is_rotor, state[:, :, 0, :], ghost_row)
    right_ghost = jnp.where(is_rotor, ghost_row, state[:, :, -1, :])
    padded_x = jnp.concatenate([left_ghost[:, :, None], state, right_ghost[:, :, None]], 2)
    flux_x = flux_along(padded_x, True)
    flux_y = flux_along(padded_y, False)
    convective = 0.5 * (flux_x[:, :, 2:] - flux_x[:, :, :-2]) + 0.5 * (
        flux_y[..., 2:] - flux_y[..., :-2]
    )
    damping = DAMPING_COEF * (
        padded_x[:, :, 2:]
        + padded_x[:, :, :-2]
        + padded_y[..., 2:]
        + padded_y[..., :-2]
        - 4.0 * state
    )
    residual = convective - damping + source
    new_state = state - PSEUDO_STEP * residual
    return (residual, new_state)


def solution(mesh):
    return jax.shard_map(
        on_device,
        mesh=mesh,
        in_specs=(
            P("inst", None, None, "cell"),
            P(None, "inst", "cell"),
            P(None, "inst", "cell"),
            P(None, "inst", "cell"),
        ),
        out_specs=(P("inst", None, None, "cell"), P("inst", None, None, "cell")),
        check_vma=False,
    )
```

profile of v0, /device:TPU:64, one launch (start us, length us, event | category | flops | bytes accessed | tf_op | source)
XLA Modules:
  0.0 166.5 jit_solution(3045347728587543568)
XLA Ops:
  7.2 0.0 copy-start
  7.2 0.0 all-gather.3.cloned.1.call-start
  7.2 0.7 all-gather.3.cloned.1.call-update
  7.9 0.5 copy-done
  8.4 0.3 fusion.39
  8.7 0.3 copy.49
  9.1 0.0 collective-permute-start
  9.1 0.3 copy.50
  9.4 1.7 %collective-permute-start.1 = (f32[1,4,512,1]{2,1,3,0:T(4,128)S(1)}, f32[1,4,512,1]{2,1,3,0:T(4,128)S(1)}, u32[]{:S(2)}, u32[]{:S(2)}) collective-permute-start(f32[1,4,512,1]{2,1,3,0:T(4,128)S(1)} %copy.50), channel_id=1, source_target_pairs={{1,0},{2,1},{3,2},{4,3},{5,4},{6,5},{7,6},{8,7},{9,8},{10,9},{11,1... | collective-permute-start | bytes 24584 | tf_op jit(solution)/shard_map/ppermute | solution.py:28
  11.1 71.2 %all-gather = f32[256,4,1,128]{3,1,2,0:T(4,128)S(1)} all-gather(f32[1,4,1,128]{3,1,2,0:T(4,128)S(1)} %broadcast_select_fusion.2), channel_id=2, replica_groups=mesh['inst'=16,'cell'=16] {'inst','cell'}, dimensions={0}, use_global_device_ids=true | all-gather | bytes 526336 | tf_op jit(solution)/shard_map/all_gather | solution.py:89
  82.3 0.0 copy-start.3
  82.3 0.0 copy-start.4
  82.3 0.0 copy-start.5
  82.3 8.6 %copy.29 = f32[16,16,1,4,128]{3,4,1,0,2:T(8,128)} copy(f32[16,16,1,4,128]{4,3,1,0,2:T(4,128)S(1)} %bitcast.126) | data formatting | bytes 1048576 | tf_op jit(solution)/shard_map/reshape | solution.py:90
  91.0 0.0 copy-done.3
  91.0 0.0 copy-done.4
  91.0 6.7 %gather_fusion.3 = f32[128,4]{1,0:T(8,128)S(1)} fusion(f32[4,32768]{0,1:T(8,128)} %bitcast.121, s32[1024]{0:T(1024)S(1)} %get-tuple-element.31), kind=kCustom, calls=%fused_computation.3.clone | custom fusion | bytes 4608 | tf_op jit(solution)/shard_map/jit(_take)/gather | solution.py:103
  97.8 0.1 copy.33
  97.8 6.7 %gather_fusion.2 = f32[128,4]{1,0:T(8,128)S(1)} fusion(f32[4,32768]{0,1:T(8,128)} %bitcast.122, s32[1024]{0:T(1024)S(1)} %get-tuple-element.32), kind=kCustom, calls=%fused_computation.2.clone | custom fusion | bytes 4608 | tf_op jit(solution)/shard_map/jit(_take)/gather | solution.py:103
  104.5 0.1 copy.32
  104.6 6.7 %gather_fusion.1 = f32[128,4]{1,0:T(8,128)S(1)} fusion(f32[4,32768]{0,1:T(8,128)} %bitcast.123, s32[1024]{0:T(1024)S(1)} %get-tuple-element.33), kind=kCustom, calls=%fused_computation.1.clone | custom fusion | bytes 4608 | tf_op jit(solution)/shard_map/jit(_take)/gather | solution.py:103
  111.3 0.1 copy.31
  111.4 6.4 %gather_fusion = f32[128,4]{1,0:T(8,128)S(1)} fusion(f32[4,32768]{0,1:T(8,128)} %bitcast.124, s32[1024]{0:T(1024)S(1)} %get-tuple-element.34), kind=kCustom, calls=%fused_computation.clone | custom fusion | bytes 4608 | tf_op jit(solution)/shard_map/jit(_take)/gather | solution.py:103
  117.8 0.1 copy.30
  117.9 0.0 copy-done.5
  118.0 0.1 pad_maximum_fusion.2
  118.1 0.1 fusion.37
  118.2 1.1 pad_maximum_fusion.3
  119.3 0.0 collective-permute-done
  119.3 0.4 copy.38
  119.7 0.0 collective-permute-done.1
  119.7 0.4 copy.39
  120.0 0.9 pad_maximum_fusion
  120.9 0.2 fusion.36
  121.2 1.5 pad_maximum_fusion.1
  122.6 7.3 %all-gather.3.cloned.1.call-done = f32[16,4,512,128]{3,2,1,0:T(8,128)} async-done(((f32[1,4,512,128]{3,2,1,0:T(8,128)}), f32[16,4,512,128]{3,2,1,0:T(8,128)}) %all-gather.3.cloned.1.call-update) | async-done | bytes 16777232 | tf_op jit(solution)/shard_map/all_gather | solution.py:96
  129.9 0.0 copy-start.1
  129.9 0.0 copy-start.2
  129.9 27.3 %fusion = f32[1,4,512,128]{3,0,2,1:T(1,128)S(1)} fusion(f32[16,4,512,128]{3,2,1,0:T(8,128)} %all-gather.3.cloned.1.call-done, f32[16,16]{1,0:T(8,128)} %constant.19.clone, s32[]{:T(128)S(6)} %select_n.50), kind=kOutput, calls=%fused_computation.4 | convolution fusion | flops 50331648 | bytes 17826308 | tf_op jit(solution)/shard_map/ij,jcxy->icxy/dot_general | solution.py:93
  157.2 0.0 copy-done.1
  157.2 0.0 copy-done.2
  157.2 2.5 %multiply_subtract_fusion = (f32[1,4,512,128]{3,2,1,0:T(8,128)}, f32[1,4,512,128]{3,2,1,0:T(8,128)}) fusion(f32[1,4,512,128]{3,2,1,0:T(8,128)S(1)} %copy-done, f32[1,4,512,128]{3,2,1,0:T(8,128)S(1)} %bitcast.125, f32[1,4,512,1]{3,2,1,0:T(8,128)S(1)} %copy.38, f32[1,4,512,1]{3,2,1,0:T(8,128)S(1)} %copy.39, f32[1,4,1,128]{3,2,1,0:T(1,128)S(1)} %bitcast.134, ...), kind=kLoop, calls=%fused_computation.25 | loop fusion | flops 4718592 | bytes 8409088 | tf_op jit(solution)/shard_map/sub | solution.py:123
  (10 shorter events, 0.1 us)
Async XLA Ops:
  7.2 1.2 copy-start
  7.2 122.7 %all-gather.3.cloned.1.call-start = ((), (), s32[]{:S(2)}) async-start(), calls=%async_computation | async-start | bytes 17825792 | tf_op jit(solution)/shard_map/all_gather | solution.py:96
  9.1 110.2 %collective-permute-start = (f32[1,4,512,1]{2,1,3,0:T(4,128)S(1)}, f32[1,4,512,1]{2,1,3,0:T(4,128)S(1)}, u32[]{:S(2)}, u32[]{:S(2)}) collective-permute-start(f32[1,4,512,1]{2,1,3,0:T(4,128)S(1)} %copy.49), channel_id=1, source_target_pairs={{0,1},{1,2},{2,3},{3,4},{4,5},{5,6},{6,7},{7,8},{8,9},{9,10},{10,1... | collective-permute-start | bytes 24584 | tf_op jit(solution)/shard_map/ppermute | solution.py:26
  9.4 110.3 %collective-permute-start.1 = (f32[1,4,512,1]{2,1,3,0:T(4,128)S(1)}, f32[1,4,512,1]{2,1,3,0:T(4,128)S(1)}, u32[]{:S(2)}, u32[]{:S(2)}) collective-permute-start(f32[1,4,512,1]{2,1,3,0:T(4,128)S(1)} %copy.50), channel_id=1, source_target_pairs={{1,0},{2,1},{3,2},{4,3},{5,4},{6,5},{7,6},{8,7},{9,8},{10,9},{11,1... | collective-permute-start | bytes 24584 | tf_op jit(solution)/shard_map/ppermute | solution.py:28
  82.3 8.6 %copy-start.3 = (s32[4,1,128]{2,1,0:T(1,128)S(1)}, s32[4,1,128]{2,1,0:T(1,128)}, u32[]{:S(2)}) copy-start(s32[4,1,128]{2,1,0:T(1,128)} %param.9) | copy-start | bytes 6148
  82.3 8.6 %copy-start.4 = (s32[4,1,128]{2,1,0:T(1,128)S(1)}, s32[4,1,128]{2,1,0:T(1,128)}, u32[]{:S(2)}) copy-start(s32[4,1,128]{2,1,0:T(1,128)} %param.8) | copy-start | bytes 6148
  82.3 35.6 %copy-start.5 = (f32[4,1,128]{2,1,0:T(1,128)S(1)}, f32[4,1,128]{2,1,0:T(1,128)}, u32[]{:S(2)}) copy-start(f32[4,1,128]{2,1,0:T(1,128)} %param.10) | copy-start | bytes 6148
  129.9 27.3 %copy-start.1 = (f32[1,4,514,128]{3,2,1,0:T(8,128)S(1)}, f32[1,4,514,128]{3,2,1,0:T(8,128)}, u32[]{:S(2)}) copy-start(f32[1,4,514,128]{3,2,1,0:T(8,128)} %pad_maximum_fusion.3) | copy-start | bytes 3158020
  129.9 27.3 %copy-start.2 = (f32[1,4,512,130]{3,2,1,0:T(8,128)S(1)}, f32[1,4,512,130]{3,2,1,0:T(8,128)}, u32[]{:S(2)}) copy-start(f32[1,4,512,130]{3,2,1,0:T(8,128)} %pad_maximum_fusion.1) | copy-start | bytes 3194884
Sparse Core Ops, SparseCore 0:
  10.4 119.4 all-gather.2
where the time goes:
time: 168 us; the launch traced here: 167 us
  blocking collectives  71.2 us (42%)
  local copies, waits for them, and re-layouts  37.7 us (22%)
  matrix products  27.3 us (16%)
  between operations  14.2 us (8%)
  waiting for transfers between devices  7.94 us (5%)
  other arithmetic  6.44 us (4%)
  starting transfers between devices  1.77 us (1%)
    all_gather x1, blocking collectives, on_device(): lax.all_gather(export[None], ('inst', 'cell'), axis=0, tiled=True)  71.2 us
    dot_general x1, matrix products, on_device(): jnp.einsum('ij,jcxy->icxy', mine, lax.all_gather(state, 'inst', axis=0, t...  27.3 us
    gather x8, local copies, waits for them, and re-layouts, on_device(): jnp.take(face_table, flat_index[entry], axis=1)  26.8 us
    reshape x1, local copies, waits for them, and re-layouts, on_device(): all_rows.reshape(inst_count, cell_count, local_inst, 4, local_width)  8.63 us
    all_gather x1, waiting for transfers between devices, on_device(): lax.all_gather(state, 'inst', axis=0, tiled=True)  7.25 us
  transfers between devices with their start and end apart: 3, of which 1 were waited for; matrix products, arithmetic and copies ran while one was open for 25% of the time, Pallas kernels for 0%

commit v1 on v0

v1 whole, which is shorter than its diff:
```python
import functools

import jax
import jax.numpy as jnp
import numpy as np
from jax import lax
from jax.experimental import pallas as pl
from jax.experimental.pallas import tpu as pltpu
from jax.sharding import PartitionSpec as P

ROTOR_INST = 9
STATOR_INST = 7
INST = ROTOR_INST + STATOR_INST
OMEGA_ROTOR = 0.8
OMEGA_STATOR = 0.6
GAMMA_LESS = 0.4
DAMPING_COEF = 0.05
PSEUDO_STEP = 0.2
LANES = 128
ROWS = 8


def pitch_coefficients(count, omega):
    steps = np.arange(1, (count - 1) // 2 + 1)
    return omega * 0.5 * np.power(-1.0, steps) / np.sin(np.pi * steps / count)


def coupled(values, omega):
    count = len(values)
    coefs = pitch_coefficients(count, omega)
    outs = []
    for i in range(count):
        total = None
        for d, coef in enumerate(coefs, 1):
            term = float(coef) * (values[(i - d) % count] - values[(i + d) % count])
            total = term if total is None else total + term
        outs.append(total)
    return outs


def source_kernel(starts_ref, gathered_ref, faces_ref, out_ref):
    depth = gathered_ref.shape[1]

    def strip(t, carry):
        rows = pl.ds(pl.multiple_of(t * ROWS, ROWS), ROWS)
        values = [gathered_ref[i, rows, :] for i in range(INST)]
        outs = coupled(values[:ROTOR_INST], OMEGA_ROTOR) + coupled(values[ROTOR_INST:], OMEGA_STATOR)
        for i in range(INST):
            out_ref[i, rows, :] = outs[i]
        return carry

    lax.fori_loop(0, depth // ROWS, strip, 0)

    lane = lax.broadcasted_iota(jnp.int32, (ROWS, LANES), 1)
    lower = lax.broadcasted_iota(jnp.int32, (ROWS, LANES), 0) < 4
    slabs = faces_ref.shape[0]
    for i in range(INST):
        start = starts_ref[i]
        slab = lax.rem(start // LANES, slabs)
        offset = lax.rem(start, LANES)
        here = faces_ref[slab]
        after = faces_ref[lax.rem(slab + 1, slabs)]
        turn0 = lax.rem(LANES - offset, LANES)
        turn1 = LANES - 1 - offset
        face0 = jnp.where(lane < LANES - offset, pltpu.roll(here, turn0, 1), pltpu.roll(after, turn0, 1))
        face1 = jnp.where(lane < LANES - 1 - offset, pltpu.roll(here, turn1, 1), pltpu.roll(after, turn1, 1))
        out_ref[i, depth : depth + ROWS, :] = jnp.where(lower, face0, face1)


def fluxes(r, m, n, e):
    inv = 1.0 / r
    a = m * inv
    b = n * inv
    ma = m * a
    mb = m * b
    nb = n * b
    p = GAMMA_LESS * (e - 0.5 * (ma + nb))
    h = e + p
    return (m, ma + p, mb, h * a), (n, mb, nb + p, h * b)


def step_kernel(
    rotor_ref, cur_ref, prev_ref, next_ref, source_ref, window_ref, right_ref, left_ref,
    inst_ref, weight_ref, residual_ref, new_ref, ghost_ref, plus_ref, minus_ref,
):
    block = pl.program_id(0)
    last = pl.num_programs(0) - 1
    size = cur_ref.shape[1]
    rotor = rotor_ref[0] > 0

    @pl.when(block == 0)
    def _():
        total = jnp.zeros((ROWS, LANES), jnp.float32)
        lower = lax.broadcasted_iota(jnp.int32, (ROWS, LANES), 0) < 4

        def spread(ref, first, second):
            return jnp.where(
                lower,
                jnp.broadcast_to(ref[first : first + 1, :], (ROWS, LANES)),
                jnp.broadcast_to(ref[second : second + 1, :], (ROWS, LANES)),
            )

        inst0, inst2 = spread(inst_ref, 0, 1), spread(inst_ref, 2, 3)
        weight0, weight2 = spread(weight_ref, 0, 1), spread(weight_ref, 2, 3)
        for i in range(INST):
            coef = jnp.where(inst0 == i, weight0, 0.0) + jnp.where(inst2 == i, weight2, 0.0)
            total = total + coef * window_ref[i // 4, i % 4]
        ghost_ref[...] = total + pltpu.roll(total, 4, 0)

    def edge(outer, own, at_end, takes_ghost):
        rows = []
        for c in range(4):
            inner = jnp.broadcast_to(own[c], (ROWS, LANES))
            ghost = jnp.broadcast_to(ghost_ref[c : c + 1, :], (ROWS, LANES))
            boundary = jnp.where(takes_ghost, ghost, inner)
            rows.append(jnp.where(at_end, boundary, outer[c]))
        return rows

    before = edge(
        [prev_ref[c] for c in range(4)],
        [cur_ref[c, 0:1, :] for c in range(4)],
        block == 0,
        jnp.logical_not(rotor),
    )
    after = edge(
        [next_ref[c] for c in range(4)],
        [cur_ref[c, size - 1 : size, :] for c in range(4)],
        block == last,
        rotor,
    )
    flux_before, _ = fluxes(*before)
    flux_after, _ = fluxes(*after)
    for c in range(4):
        minus_ref[c, 0:ROWS, :] = 0.5 * flux_before[c] + DAMPING_COEF * before[c]
        plus_ref[c, size + ROWS : size + 2 * ROWS, :] = 0.5 * flux_after[c] - DAMPING_COEF * after[c]

    lane = lax.broadcasted_iota(jnp.int32, (ROWS, LANES), 1)

    def first(t, carry):
        rows = pl.ds(pl.multiple_of(t * ROWS, ROWS), ROWS)
        shifted = pl.ds(pl.multiple_of(t * ROWS + ROWS, ROWS), ROWS)
        u = [cur_ref[c, rows, :] for c in range(4)]
        flux_x, flux_y = fluxes(*u)
        for c in range(4):
            half_x = 0.5 * flux_x[c]
            half_y = 0.5 * flux_y[c]
            damped = DAMPING_COEF * u[c]
            plus_ref[c, shifted, :] = half_x - damped
            minus_ref[c, shifted, :] = half_x + damped
            up = jnp.where(lane == 0, right_ref[c, rows, :], half_y - damped)
            down = jnp.where(lane == LANES - 1, left_ref[c, rows, :], half_y + damped)
            residual_ref[c, rows, :] = (
                pltpu.roll(up, LANES - 1, 1)
                - pltpu.roll(down, 1, 1)
                + (4.0 * DAMPING_COEF) * u[c]
                + source_ref[c, 0, rows, :]
            )
        return carry

    lax.fori_loop(0, size // ROWS, first, 0)

    for t in range(size // ROWS):
        lo = t * ROWS
        for c in range(4):
            out = (
                residual_ref[c, lo : lo + ROWS, :]
                + plus_ref[c, lo + ROWS + 1 : lo + 2 * ROWS + 1, :]
                - minus_ref[c, lo + ROWS - 1 : lo + 2 * ROWS - 1, :]
            )
            residual_ref[c, lo : lo + ROWS, :] = out
            new_ref[c, lo : lo + ROWS, :] = cur_ref[c, lo : lo + ROWS, :] - PSEUDO_STEP * out


def on_device(state, src_inst, src_face, weights):
    cells = state[0]
    axial, width = cells.shape[1], cells.shape[2]
    inst_count = lax.axis_size("inst")
    cell_count = lax.axis_size("cell")
    rotor = lax.axis_index("inst") < ROTOR_INST
    depth = 4 * axial // inst_count

    export = jnp.where(rotor, cells[:, -1, :], cells[:, 0, :])
    faces = lax.all_gather(jnp.concatenate([export, export], 0), "cell", axis=0)
    starts = lax.all_gather(src_face[0, 0, :1], "inst", axis=0, tiled=True)

    head, tail = cells[:, :, 0], cells[:, :, width - 1]
    _, head_flux = fluxes(*head)
    _, tail_flux = fluxes(*tail)
    head = 0.5 * jnp.stack(head_flux) - DAMPING_COEF * head
    tail = 0.5 * jnp.stack(tail_flux) + DAMPING_COEF * tail
    right = lax.ppermute(head, "cell", [((i + 1) % cell_count, i) for i in range(cell_count)])
    left = lax.ppermute(tail, "cell", [(i, (i + 1) % cell_count) for i in range(cell_count)])

    gathered = lax.all_to_all(cells.reshape(inst_count, depth, width), "inst", 0, 0)
    packed = pl.pallas_call(
        source_kernel,
        out_shape=jax.ShapeDtypeStruct((inst_count, depth + ROWS, width), jnp.float32),
        in_specs=[
            pl.BlockSpec(memory_space=pltpu.SMEM),
            pl.BlockSpec(memory_space=pltpu.VMEM),
            pl.BlockSpec(memory_space=pltpu.VMEM),
        ],
        out_specs=pl.BlockSpec(memory_space=pltpu.VMEM),
        compiler_params=pltpu.CompilerParams(vmem_limit_bytes=16 << 20),
        name="source",
    )(starts, gathered, faces)
    packed = lax.all_to_all(packed, "inst", 0, 0).reshape(4, inst_count // 4, depth + ROWS, width)

    blocks = axial // depth
    per = depth // ROWS
    strips = axial // ROWS
    block_spec = pl.BlockSpec((4, depth, width), lambda g: (0, g, 0))
    halo_spec = pl.BlockSpec((4, depth, 1), lambda g: (0, g, 0))
    residual, new_state = pl.pallas_call(
        step_kernel,
        grid=(blocks,),
        out_shape=[jax.ShapeDtypeStruct(cells.shape, jnp.float32)] * 2,
        in_specs=[
            pl.BlockSpec(memory_space=pltpu.SMEM),
            block_spec,
            pl.BlockSpec((4, ROWS, width), lambda g: (0, jnp.maximum(g * per - 1, 0), 0)),
            pl.BlockSpec((4, ROWS, width), lambda g: (0, jnp.minimum(g * per + per, strips - 1), 0)),
            pl.BlockSpec((4, 1, depth, width), lambda g: (0, g, 0, 0)),
            pl.BlockSpec((4, inst_count // 4, ROWS, width), lambda g: (0, 0, per, 0)),
            halo_spec,
            halo_spec,
            pl.BlockSpec((4, width), lambda g: (0, 0)),
            pl.BlockSpec((4, width), lambda g: (0, 0)),
        ],
        out_specs=[block_spec, block_spec],
        scratch_shapes=[
            pltpu.VMEM((ROWS, width), jnp.float32),
            pltpu.VMEM((4, depth + 2 * ROWS, width), jnp.float32),
            pltpu.VMEM((4, depth + 2 * ROWS, width), jnp.float32),
        ],
        compiler_params=pltpu.CompilerParams(vmem_limit_bytes=16 << 20),
        name="step",
    )(
        rotor.astype(jnp.int32)[None],
        cells, cells, cells, packed, packed, right[:, :, None], left[:, :, None],
        src_inst[:, 0, :], weights[:, 0, :],
    )
    return residual[None], new_state[None]


def solution(mesh):
    return jax.shard_map(
        on_device,
        mesh=mesh,
        in_specs=(
            P("inst", None, None, "cell"),
            P(None, "inst", "cell"),
            P(None, "inst", "cell"),
            P(None, "inst", "cell"),
        ),
        out_specs=(P("inst", None, None, "cell"), P("inst", None, None, "cell")),
        check_vma=False,
    )
```

time: 168 us -> 93.6 us (0.56)
  the two profiles are of different devices: /device:TPU:64 before, /device:TPU:1 now
where the time goes in v1:
time: 93.6 us; the launch traced here: 93.2 us
  blocking collectives  43.1 us (46%)
  waiting for transfers between devices  16.1 us (17%)
  Pallas kernels  13.4 us (14%)
  starting transfers between devices  11.9 us (13%)
  local copies, waits for them, and re-layouts  6.03 us (6%)
  other arithmetic  1.91 us (2%)
    all_gather x1, blocking collectives, on_device(): faces = lax.all_gather(jnp.concatenate([export, export], 0), 'cell', axis=0)  24.1 us
    all_gather x1, blocking collectives, on_device(): starts = lax.all_gather(src_face[0, 0, :1], 'inst', axis=0, tiled=True)  18.9 us
    all_to_all x1, waiting for transfers between devices, on_device(): lax.all_to_all(packed, 'inst', 0, 0)  13.9 us
    pallas_call x1, Pallas kernels, on_device(): pl.pallas_call(step_kernel, grid=(blocks,), out_shape=[jax.ShapeDtypeStru...  11.2 us
    all_to_all x1, starting transfers between devices, on_device(): lax.all_to_all(cells.reshape(inst_count, depth, width), 'inst', 0, 0)  7.73 us
    all_to_all x1, starting transfers between devices, on_device(): lax.all_to_all(packed, 'inst', 0, 0)  3.7 us
    unnamed x13, local copies, waits for them, and re-layouts  3.15 us
    pallas_call x1, Pallas kernels, on_device(): pl.pallas_call(source_kernel, out_shape=jax.ShapeDtypeStruct((inst_count,...  2.21 us
  transfers between devices with their start and end apart: 4, of which 3 were waited for; matrix products, arithmetic and copies ran while one was open for 7% of the time, Pallas kernels for 0%

profile of v1, /device:TPU:1, one launch (start us, length us, event | category | flops | bytes accessed | tf_op | source)
XLA Modules:
  0.0 93.2 jit_solution(2712344197384662983)
XLA Ops:
  0.6 0.0 copy-start.4
  0.6 0.0 copy-start
  0.7 7.7 %all-to-all-start = ((f32[16,128,128]{2,1,0:T(8,128)}), f32[16,128,128]{2,1,0:T(8,128)S(1)}, u32[]{:S(2)}, u32[]{:S(2)}) async-start(f32[16,128,128]{2,1,0:T(8,128)} %bitcast.23), calls=%async_computation | async-start | bytes 2097152 | tf_op jit(solution)/shard_map/all_to_all | solution.py:194
  8.4 1.2 %slice.31 = s32[1,1,1]{2,1,0:T(1,128)} slice(s32[4,1,128]{2,1,0:T(1,128)} %param.6), slice={[0:1], [0:1], [0:1]} | slice | bytes 8 | tf_op jit(solution)/shard_map/slice | solution.py:184
  9.6 0.0 copy-done.4
  9.6 0.6 dynamic-slice
  10.2 1.3 %bitcast_dynamic-update-slice_fusion = s32[16]{0:T(128)S(1)} fusion(s32[16]{0:T(128)S(1)} %broadcast.102, u32[]{:T(128)} %bitcast.3, s32[1,1,1]{2,1,0:T(1,128)} %slice.31), kind=kLoop, calls=%fused_computation.28 | loop fusion | bytes 72
  11.5 18.9 %all-reduce.starts_ref = s32[16]{0:T(128)S(1)} all-reduce(s32[16]{0:T(128)S(1)} %bitcast_dynamic-update-slice_fusion), channel_id=2, replica_groups=mesh['inst'=16,'cell'=16] {'inst'}, use_global_device_ids=true, to_apply=%add | all-reduce | flops 16 | bytes 128 | tf_op jit(solution)/shard_map/all_gather | solution.py:184
  30.4 0.0 copy-done
  30.4 24.1 %all-gather.1 = f32[128,128]{1,0:T(8,128)S(1)} all-gather(f32[8,128]{1,0:T(8,128)S(1)} %pad_maximum_fusion), channel_id=3, replica_groups=mesh['inst'=16,'cell'=16] {'cell'}, dimensions={0}, use_global_device_ids=true | all-gather | bytes 69632 | tf_op jit(solution)/shard_map/all_gather | solution.py:183
  54.6 0.9 slice_reduce_fusion.1
  55.5 0.0 all-to-all-done.gathered_ref
  55.5 2.2 %source.1 = f32[16,136,128]{2,1,0:T(8,128)} custom-call(s32[16]{0:T(128)S(1)} %all-reduce.starts_ref, f32[16,128,128]{2,1,0:T(8,128)S(1)} %all-to-all-done.gathered_ref, f32[16,8,128]{2,1,0:T(8,128)S(1)} %bitcast.32), custom_call_target="tpu_custom_call" | custom-call | tf_op jit(solution)/shard_map/source/pallas_call | solution.py:195
  57.7 3.7 %all-to-all-start.1 = ((f32[16,136,128]{2,1,0:T(8,128)}), f32[16,136,128]{2,1,0:T(8,128)S(1)}, u32[]{:S(2)}, u32[]{:S(2)}) async-start(f32[16,136,128]{2,1,0:T(8,128)} %source.1), calls=%async_computation.1 | async-start | bytes 2228224 | tf_op jit(solution)/shard_map/all_to_all | solution.py:207
  61.4 0.9 fusion
  62.3 0.0 copy-start.2
  62.3 0.0 copy-start.3
  62.4 0.0 collective-permute-start.1
  62.5 0.5 collective-permute-start
  63.0 0.6 collective-permute-done.1
  63.6 0.4 copy.25.left_ref
  63.9 1.6 %collective-permute-done = f32[4,512]{1,0:T(4,128)S(1)} collective-permute-done((f32[4,512]{1,0:T(4,128)S(1)}, f32[4,512]{1,0:T(4,128)S(1)}, u32[]{:S(2)}, u32[]{:S(2)}) %collective-permute-start) | collective-permute-done | bytes 8224 | tf_op jit(solution)/shard_map/ppermute | solution.py:191
  65.5 1.3 %copy.24.right_ref = f32[4,512,1]{2,1,0:T(8,128)} copy(f32[4,512,1]{1,0,2:T(4,128)S(1)} %bitcast.40) | data formatting | bytes 16384 | tf_op jit(solution)/shard_map/broadcast_in_dim | solution.py:240
  66.9 13.9 %all-to-all-done.1 = f32[16,136,128]{2,1,0:T(8,128)S(1)} async-done(((f32[16,136,128]{2,1,0:T(8,128)}), f32[16,136,128]{2,1,0:T(8,128)S(1)}, u32[]{:S(2)}, u32[]{:S(2)}) %all-to-all-start.1) | async-done | bytes 1114144 | tf_op jit(solution)/shard_map/all_to_all | solution.py:207
  80.8 0.0 copy-done.2
  80.8 0.0 copy-done.3
  80.8 0.0 copy-start.1
  80.8 1.2 %copy-done.1 = f32[4,512,1]{2,1,0:T(8,128)S(1)} copy-done((f32[4,512,1]{2,1,0:T(8,128)S(1)}, f32[4,512,1]{2,1,0:T(8,128)}, u32[]{:S(2)}) %copy-start.1) | copy-done | bytes 8216
  82.0 11.2 %step.1 = (f32[4,512,128]{2,1,0:T(8,128)}, f32[4,512,128]{2,1,0:T(8,128)}) custom-call(s32[1]{0:T(128)} %bitcast.rotor_ref, f32[4,512,128]{2,1,0:T(8,128)S(1)} %bitcast.27, f32[4,512,128]{2,1,0:T(8,128)S(1)} %bitcast.28, f32[4,512,128]{2,1,0:T(8,128)S(1)} %bitcast.29, f32[4,4,136,128]{3,2,1,0:T(8,128)S(1)} %bitcast.30, f32[4,4,136,128]{3,2,1,0:T(8,128)S(1)} %bitcast.31, ...), custom_call_target="tpu_custom_call" | custom-call | tf_op jit(solution)/shard_map/step/pallas_call | solution.py:214
  (7 shorter events, 0.1 us)
Async XLA Ops:
  0.6 8.9 %copy-start.4 = (u32[256]{0:T(256)S(1)}, u32[256]{0:T(256)}, u32[]{:S(2)}) copy-start(u32[256]{0:T(256)} %constant.22) | copy-start | bytes 3076
  0.6 29.8 %copy-start = (f32[1,4,512,128]{3,2,1,0:T(8,128)S(1)}, f32[1,4,512,128]{3,2,1,0:T(8,128)}, u32[]{:S(2)}) copy-start(f32[1,4,512,128]{3,2,1,0:T(8,128)} %param.4) | copy-start | bytes 3145732
  0.7 54.8 %all-to-all-start = ((f32[16,128,128]{2,1,0:T(8,128)}), f32[16,128,128]{2,1,0:T(8,128)S(1)}, u32[]{:S(2)}, u32[]{:S(2)}) async-start(f32[16,128,128]{2,1,0:T(8,128)} %bitcast.23), calls=%async_computation | async-start | bytes 2097152 | tf_op jit(solution)/shard_map/all_to_all | solution.py:194
  57.7 23.1 %all-to-all-start.1 = ((f32[16,136,128]{2,1,0:T(8,128)}), f32[16,136,128]{2,1,0:T(8,128)S(1)}, u32[]{:S(2)}, u32[]{:S(2)}) async-start(f32[16,136,128]{2,1,0:T(8,128)} %source.1), calls=%async_computation.1 | async-start | bytes 2228224 | tf_op jit(solution)/shard_map/all_to_all | solution.py:207
  62.3 18.4 %copy-start.2 = (s32[4,1,128]{2,1,0:T(1,128)S(1)}, s32[4,1,128]{2,1,0:T(1,128)}, u32[]{:S(2)}) copy-start(s32[4,1,128]{2,1,0:T(1,128)} %param.5) | copy-start | bytes 6148
  62.3 18.4 %copy-start.3 = (f32[4,1,128]{2,1,0:T(1,128)S(1)}, f32[4,1,128]{2,1,0:T(1,128)}, u32[]{:S(2)}) copy-start(f32[4,1,128]{2,1,0:T(1,128)} %param.7) | copy-start | bytes 6148
  62.4 1.2 %collective-permute-start.1 = (f32[4,512]{1,0:T(4,128)S(1)}, f32[4,512]{1,0:T(4,128)S(1)}, u32[]{:S(2)}, u32[]{:S(2)}) collective-permute-start(f32[4,512]{1,0:T(4,128)S(1)} %fusion.5), channel_id=1, source_target_pairs={{0,1},{1,2},{2,3},{3,4},{4,5},{5,6},{6,7},{7,8},{8,9},{9,10},{10,1... | collective-permute-start | bytes 24584 | tf_op jit(solution)/shard_map/ppermute | solution.py:192
  62.5 3.1 %collective-permute-start = (f32[4,512]{1,0:T(4,128)S(1)}, f32[4,512]{1,0:T(4,128)S(1)}, u32[]{:S(2)}, u32[]{:S(2)}) collective-permute-start(f32[4,512]{1,0:T(4,128)S(1)} %fusion.4), channel_id=1, source_target_pairs={{1,0},{2,1},{3,2},{4,3},{5,4},{6,5},{7,6},{8,7},{9,8},{10,9},{11,1... | collective-permute-start | bytes 24584 | tf_op jit(solution)/shard_map/ppermute | solution.py:191
  80.8 1.2 %copy-start.1 = (f32[4,512,1]{2,1,0:T(8,128)S(1)}, f32[4,512,1]{2,1,0:T(8,128)}, u32[]{:S(2)}) copy-start(f32[4,512,1]{2,1,0:T(8,128)} %copy.24.right_ref) | copy-start | bytes 24580

commit v2 on v1

v2 whole, which is shorter than its diff:
```python
import jax
import jax.numpy as jnp
import numpy as np
from jax import lax
from jax.experimental import pallas as pl
from jax.experimental.pallas import tpu as pltpu
from jax.sharding import PartitionSpec as P

ROTOR_INST = 9
STATOR_INST = 7
INST = ROTOR_INST + STATOR_INST
OMEGA_ROTOR = 0.8
OMEGA_STATOR = 0.6
GAMMA_LESS = 0.4
DAMPING_COEF = 0.05
PSEUDO_STEP = 0.2
LANES = 128
ROWS = 8


def pitch_coefficients(count, omega):
    steps = np.arange(1, (count - 1) // 2 + 1)
    return omega * 0.5 * np.power(-1.0, steps) / np.sin(np.pi * steps / count)


def coupled(values, omega):
    count = len(values)
    coefs = pitch_coefficients(count, omega)
    outs = []
    for i in range(count):
        total = None
        for d, coef in enumerate(coefs, 1):
            term = float(coef) * (values[(i - d) % count] - values[(i + d) % count])
            total = term if total is None else total + term
        outs.append(total)
    return outs


def send_kernel(cells_ref, face_ref, out_ref, want_ref, sems):
    depth = out_ref.shape[1] - ROWS
    asked = pltpu.make_async_copy(face_ref, want_ref, sems.at[0])
    asked.start()
    chunks = pltpu.make_async_copy(cells_ref, out_ref.at[:, pl.ds(0, depth), :], sems.at[1])
    chunks.start()
    asked.wait()
    lower = lax.broadcasted_iota(jnp.int32, (ROWS, LANES), 0) < 4
    want = jnp.where(
        lower,
        jnp.broadcast_to(want_ref[0], (ROWS, LANES)),
        jnp.broadcast_to(want_ref[1], (ROWS, LANES)),
    ).astype(jnp.float32)
    for j in range(out_ref.shape[0]):
        out_ref[j, depth : depth + ROWS, :] = want
    chunks.wait()


def source_kernel(gathered_ref, faces_ref, out_ref):
    depth = gathered_ref.shape[1] - ROWS
    slab = lax.axis_index("cell")

    def strip(t, carry):
        rows = pl.ds(pl.multiple_of(t * ROWS, ROWS), ROWS)
        values = [gathered_ref[i, rows, :] for i in range(INST)]
        outs = coupled(values[:ROTOR_INST], OMEGA_ROTOR) + coupled(values[ROTOR_INST:], OMEGA_STATOR)
        for i in range(INST):
            out_ref[i, rows, :] = outs[i]
        return carry

    lax.fori_loop(0, depth // ROWS, strip, 0, unroll=2)

    slabs = faces_ref.shape[0] // ROWS
    wants = [gathered_ref[i, depth : depth + ROWS, :].astype(jnp.int32) for i in range(INST)]
    firsts = [(want[0, 0] >> 7) & (slabs - 1) for want in wants]
    windows = []
    for want, first in zip(wants, firsts):
        ahead = (first - slab) & (slabs - 1)
        here = faces_ref[pl.ds(pl.multiple_of(ahead * ROWS, ROWS), ROWS), :]
        ahead = (ahead + 1) & (slabs - 1)
        after = faces_ref[pl.ds(pl.multiple_of(ahead * ROWS, ROWS), ROWS), :]
        place = want & (LANES - 1)
        here = jnp.take_along_axis(here, place, axis=1, mode="promise_in_bounds")
        after = jnp.take_along_axis(after, place, axis=1, mode="promise_in_bounds")
        windows.append(jnp.where((want >> 7) == first, here, after))
    for i in range(INST):
        out_ref[i, depth : depth + ROWS, :] = windows[i]


def fluxes(r, m, n, e):
    inv = 1.0 / r
    a = m * inv
    b = n * inv
    ma = m * a
    mb = m * b
    nb = n * b
    p = GAMMA_LESS * (e - 0.5 * (ma + nb))
    h = e + p
    return (m, ma + p, mb, h * a), (n, mb, nb + p, h * b)


def partial_kernel(
    cur_ref, prev_ref, next_ref, right_ref, left_ref, out_ref, plus_ref, minus_ref
):
    block = pl.program_id(0)
    last = pl.num_programs(0) - 1
    size = cur_ref.shape[1]
    rotor = lax.axis_index("inst") < ROTOR_INST

    def edge(outer, own, at_end):
        return [jnp.where(at_end, jnp.broadcast_to(own[c], (ROWS, LANES)), outer[c]) for c in range(4)]

    before = edge([prev_ref[c] for c in range(4)], [cur_ref[c, 0:1, :] for c in range(4)], block == 0)
    after = edge(
        [next_ref[c] for c in range(4)], [cur_ref[c, size - 1 : size, :] for c in range(4)], block == last
    )
    keep_before = jnp.where(jnp.logical_or(block > 0, rotor), 1.0, 0.0)
    keep_after = jnp.where(jnp.logical_and(block == last, rotor), 0.0, 1.0)
    flux_before, _ = fluxes(*before)
    flux_after, _ = fluxes(*after)
    for c in range(4):
        minus_ref[c, 0:ROWS, :] = keep_before * (0.5 * flux_before[c] + DAMPING_COEF * before[c])
        plus_ref[c, size + ROWS : size + 2 * ROWS, :] = keep_after * (
            0.5 * flux_after[c] - DAMPING_COEF * after[c]
        )

    lane = lax.broadcasted_iota(jnp.int32, (ROWS, LANES), 1)

    def first(t, carry):
        rows = pl.ds(pl.multiple_of(t * ROWS, ROWS), ROWS)
        shifted = pl.ds(pl.multiple_of(t * ROWS + ROWS, ROWS), ROWS)
        u = [cur_ref[c, rows, :] for c in range(4)]
        flux_x, flux_y = fluxes(*u)
        for c in range(4):
            half_x = 0.5 * flux_x[c]
            half_y = 0.5 * flux_y[c]
            damped = DAMPING_COEF * u[c]
            plus_ref[c, shifted, :] = half_x - damped
            minus_ref[c, shifted, :] = half_x + damped
            up = jnp.where(lane == 0, right_ref[c, rows, :], half_y - damped)
            down = jnp.where(lane == LANES - 1, left_ref[c, rows, :], half_y + damped)
            out_ref[c, rows, :] = (
                pltpu.roll(up, LANES - 1, 1) - pltpu.roll(down, 1, 1) + (4.0 * DAMPING_COEF) * u[c]
            )
        return carry

    lax.fori_loop(0, size // ROWS, first, 0, unroll=4)

    for t in range(size // ROWS):
        lo = t * ROWS
        for c in range(4):
            out_ref[c, lo : lo + ROWS, :] = (
                out_ref[c, lo : lo + ROWS, :]
                + plus_ref[c, lo + ROWS + 1 : lo + 2 * ROWS + 1, :]
                - minus_ref[c, lo + ROWS - 1 : lo + 2 * ROWS - 1, :]
            )


def finish_kernel(
    packed_ref, partial_ref, cells_ref, inst_ref, weight_ref, residual_ref, new_ref, res_ref, next_ref, sems
):
    rotor = lax.axis_index("inst") < ROTOR_INST
    axial = cells_ref.shape[1]
    depth = packed_ref.shape[1] - ROWS
    per = axial // depth
    row = lax.broadcasted_iota(jnp.int32, (ROWS, LANES), 0)
    lower = row < 4

    def spread(ref, first, second):
        return jnp.where(
            lower,
            jnp.broadcast_to(ref[first : first + 1, :], (ROWS, LANES)),
            jnp.broadcast_to(ref[second : second + 1, :], (ROWS, LANES)),
        )

    inst0, inst2 = spread(inst_ref, 0, 1), spread(inst_ref, 2, 3)
    weight0, weight2 = spread(weight_ref, 0, 1), spread(weight_ref, 2, 3)
    total = jnp.zeros((ROWS, LANES), jnp.float32)
    for i in range(INST):
        coef = jnp.where(inst0 == i, weight0, 0.0) + jnp.where(inst2 == i, weight2, 0.0)
        total = total + coef * packed_ref[i, depth : depth + ROWS, :]
    ghost = total + pltpu.roll(total, 4, 0)
    ghost = [jnp.broadcast_to(ghost[c : c + 1, :], (ROWS, LANES)) for c in range(4)]
    flux_x, _ = fluxes(*ghost)
    head = jnp.logical_and(row == 0, jnp.logical_not(rotor))
    tail = jnp.logical_and(row == ROWS - 1, rotor)
    copies = []
    for c in range(4):
        half, damped = 0.5 * flux_x[c], DAMPING_COEF * ghost[c]
        at_head = jnp.where(head, -half - damped, 0.0)
        at_tail = jnp.where(tail, half - damped, 0.0)
        for j in range(per):

            def strip(t, carry, c=c, j=j):
                rows = pl.ds(pl.multiple_of(j * depth + t * ROWS, ROWS), ROWS)
                mine = pl.ds(pl.multiple_of(t * ROWS, ROWS), ROWS)
                out = partial_ref[c, rows, :] + packed_ref[c * per + j, mine, :]
                res_ref[c, rows, :] = out
                next_ref[c, rows, :] = cells_ref[c, rows, :] - PSEUDO_STEP * out
                return carry

            lax.fori_loop(0, depth // ROWS, strip, 0, unroll=True)
        for first, extra in ((0, at_head), (axial - ROWS, at_tail)):
            out = res_ref[c, first : first + ROWS, :] + extra
            res_ref[c, first : first + ROWS, :] = out
            next_ref[c, first : first + ROWS, :] = cells_ref[c, first : first + ROWS, :] - PSEUDO_STEP * out
        for k, (src, dst) in enumerate(((res_ref, residual_ref), (next_ref, new_ref))):
            copy = pltpu.make_async_copy(src.at[c], dst.at[c], sems.at[2 * c + k])
            copy.start()
            copies.append(copy)
    for copy in copies:
        copy.wait()


def collected(block, axis):
    count = lax.axis_size(axis)
    step = 1
    while step < count:
        pairs = [((i + step) % count, i) for i in range(count)]
        block = jnp.concatenate([block, lax.ppermute(block, axis, pairs)], 0)
        step *= 2
    return block


def on_device(state, src_inst, src_face, weights):
    cells = state[0]
    axial, width = cells.shape[1], cells.shape[2]
    inst_count = lax.axis_size("inst")
    cell_count = lax.axis_size("cell")
    rotor = lax.axis_index("inst") < ROTOR_INST
    depth = 4 * axial // inst_count

    vmem = pl.BlockSpec(memory_space=pltpu.VMEM)
    anywhere = pl.BlockSpec(memory_space=pl.ANY)
    sent = pl.pallas_call(
        send_kernel,
        out_shape=pltpu.VMEM((inst_count, depth + ROWS, width), jnp.float32),
        in_specs=[anywhere, anywhere],
        out_specs=vmem,
        scratch_shapes=[pltpu.VMEM(src_face.shape, jnp.int32), pltpu.SemaphoreType.DMA((2,))],
        compiler_params=pltpu.CompilerParams(vmem_limit_bytes=16 << 20),
        name="send",
    )(cells.reshape(inst_count, depth, width), src_face)
    gathered = lax.all_to_all(sent, "inst", 0, 0)
    export = jnp.where(rotor, cells[:, -1, :], cells[:, 0, :])
    faces = collected(jnp.concatenate([export, export], 0), "cell")
    packed = pl.pallas_call(
        source_kernel,
        out_shape=pltpu.VMEM((inst_count, depth + ROWS, width), jnp.float32),
        in_specs=[vmem, vmem],
        out_specs=vmem,
        compiler_params=pltpu.CompilerParams(vmem_limit_bytes=16 << 20),
        name="source",
    )(gathered, faces)
    cells, packed = lax.optimization_barrier((cells, packed))
    packed = lax.all_to_all(packed, "inst", 0, 0)

    head, tail = cells[:, :, 0], cells[:, :, width - 1]
    _, head_flux = fluxes(*head)
    _, tail_flux = fluxes(*tail)
    head = 0.5 * jnp.stack(head_flux) - DAMPING_COEF * head
    tail = 0.5 * jnp.stack(tail_flux) + DAMPING_COEF * tail
    right = lax.ppermute(head, "cell", [((i + 1) % cell_count, i) for i in range(cell_count)])
    left = lax.ppermute(tail, "cell", [(i, (i + 1) % cell_count) for i in range(cell_count)])

    blocks = axial // depth
    per = depth // ROWS
    strips = axial // ROWS
    block_spec = pl.BlockSpec((4, depth, width), lambda g: (0, g, 0))
    halo_spec = pl.BlockSpec((4, depth, 1), lambda g: (0, g, 0))
    partial = pl.pallas_call(
        partial_kernel,
        grid=(blocks,),
        out_shape=pltpu.VMEM(cells.shape, jnp.float32),
        in_specs=[
            block_spec,
            pl.BlockSpec((4, ROWS, width), lambda g: (0, jnp.maximum(g * per - 1, 0), 0)),
            pl.BlockSpec((4, ROWS, width), lambda g: (0, jnp.minimum(g * per + per, strips - 1), 0)),
            halo_spec,
            halo_spec,
        ],
        out_specs=block_spec,
        scratch_shapes=[
            pltpu.VMEM((4, depth + 2 * ROWS, width), jnp.float32),
            pltpu.VMEM((4, depth + 2 * ROWS, width), jnp.float32),
        ],
        compiler_params=pltpu.CompilerParams(vmem_limit_bytes=16 << 20),
        cost_estimate=pl.CostEstimate(flops=100 * cells.size, bytes_accessed=16 * cells.size, transcendentals=0),
        name="partial",
    )(cells, cells, cells, right[:, :, None], left[:, :, None])
    residual, new_state = pl.pallas_call(
        finish_kernel,
        out_shape=[jax.ShapeDtypeStruct(cells.shape, jnp.float32)] * 2,
        in_specs=[vmem] * 5,
        out_specs=[anywhere, anywhere],
        scratch_shapes=[
            pltpu.VMEM(cells.shape, jnp.float32),
            pltpu.VMEM(cells.shape, jnp.float32),
            pltpu.SemaphoreType.DMA((8,)),
        ],
        compiler_params=pltpu.CompilerParams(vmem_limit_bytes=16 << 20),
        name="finish",
    )(packed, partial, cells, src_inst[:, 0, :], weights[:, 0, :])
    return residual[None], new_state[None]


def solution(mesh):
    return jax.shard_map(
        on_device,
        mesh=mesh,
        in_specs=(
            P("inst", None, None, "cell"),
            P(None, "inst", "cell"),
            P(None, "inst", "cell"),
            P(None, "inst", "cell"),
        ),
        out_specs=(P("inst", None, None, "cell"), P("inst", None, None, "cell")),
        check_vma=False,
    )
```

time: 93.6 us -> 63.1 us (0.67)
  the two profiles are of different devices: /device:TPU:1 before, /device:TPU:96 now
where the time goes in v2:
time: 63.1 us; the launch traced here: 62.7 us
  waiting for transfers between devices  23.1 us (37%)
  starting transfers between devices  22.3 us (35%)
  Pallas kernels  7.51 us (12%)
  local copies, waits for them, and re-layouts  7.1 us (11%)
  other arithmetic  1.93 us (3%)
  between operations  0.75 us (1%)
    ppermute x4, waiting for transfers between devices, collected(): block = jnp.concatenate([block, lax.ppermute(block, axis, pairs)], 0)  13.9 us
    all_to_all x1, waiting for transfers between devices, on_device(): packed = lax.all_to_all(packed, 'inst', 0, 0)  7.89 us
    all_to_all x1, starting transfers between devices, on_device(): packed = lax.all_to_all(packed, 'inst', 0, 0)  7.22 us
    all_to_all x1, starting transfers between devices, on_device(): gathered = lax.all_to_all(sent, 'inst', 0, 0)  7.18 us
    ppermute x4, starting transfers between devices, collected(): block = jnp.concatenate([block, lax.ppermute(block, axis, pairs)], 0)  6.12 us
    unnamed x14, local copies, waits for them, and re-layouts  4.36 us
    pallas_call x1, Pallas kernels, on_device(): pl.pallas_call(partial_kernel, grid=(blocks,), out_shape=pltpu.VMEM(cells...  3.45 us
    pallas_call x1, Pallas kernels, on_device(): pl.pallas_call(source_kernel, out_shape=pltpu.VMEM((inst_count, depth + R...  1.54 us
  transfers between devices with their start and end apart: 8, of which 6 were waited for; matrix products, arithmetic and copies ran while one was open for 7% of the time, Pallas kernels for 6%

profile of v2, /device:TPU:96, one launch (start us, length us, event | category | flops | bytes accessed | tf_op | source)
XLA Modules:
  0.0 62.7 jit_solution(5541144273547731302)
XLA Ops:
  0.6 0.0 copy-start
  0.6 1.2 %copy-done = f32[1,4,512,128]{3,2,1,0:T(8,128)S(1)} copy-done((f32[1,4,512,128]{3,2,1,0:T(8,128)S(1)}, f32[1,4,512,128]{3,2,1,0:T(8,128)}, u32[]{:S(2)}) %copy-start) | copy-done | bytes 1048600
  1.9 0.0 copy-start.4
  1.9 0.7 %copy-done.4 = s32[4,1,128]{2,1,0:T(1,128)S(1)} copy-done((s32[4,1,128]{2,1,0:T(1,128)S(1)}, s32[4,1,128]{2,1,0:T(1,128)}, u32[]{:S(2)}) %copy-start.4) | copy-done | bytes 2072
  2.5 1.1 %send.1 = f32[16,136,128]{2,1,0:T(8,128)} custom-call(f32[16,128,128]{2,1,0:T(8,128)S(1)} %bitcast.17, s32[4,1,128]{2,1,0:T(1,128)S(1)} %copy-done.4), custom_call_target="tpu_custom_call" | custom-call | tf_op jit(solution)/shard_map/send/pallas_call | solution.py:233
  3.6 0.0 copy-start.1
  3.6 7.2 %all-to-all-start = ((f32[16,136,128]{2,1,0:T(8,128)}), f32[16,136,128]{2,1,0:T(8,128)S(1)}, u32[]{:S(2)}, u32[]{:S(2)}) async-start(f32[16,136,128]{2,1,0:T(8,128)} %send.1), calls=%async_computation | async-start | bytes 2228224 | tf_op jit(solution)/shard_map/all_to_all | solution.py:242
  10.8 0.0 copy-done.1
  10.9 0.0 collective-permute-start
  10.9 1.3 %collective-permute-done = f32[8,128]{1,0:T(8,128)S(1)} collective-permute-done((f32[8,128]{1,0:T(8,128)S(1)}, f32[8,128]{1,0:T(8,128)S(1)}, u32[]{:S(2)}, u32[]{:S(2)}) %collective-permute-start) | collective-permute-done | bytes 4128 | tf_op jit(solution)/shard_map/ppermute | solution.py:218
  12.2 0.1 collective-permute-start.1
  12.3 4.8 %collective-permute-done.1 = f32[16,128]{1,0:T(8,128)S(1)} collective-permute-done((f32[16,128]{1,0:T(8,128)S(1)}, f32[16,128]{1,0:T(8,128)S(1)}, u32[]{:S(2)}, u32[]{:S(2)}) %collective-permute-start.1) | collective-permute-done | bytes 8224 | tf_op jit(solution)/shard_map/ppermute | solution.py:218
  17.1 1.3 %collective-permute-start.2 = (f32[32,128]{1,0:T(8,128)S(1)}, f32[32,128]{1,0:T(8,128)S(1)}, u32[]{:S(2)}, u32[]{:S(2)}) collective-permute-start(f32[32,128]{1,0:T(8,128)S(1)} %pad_maximum_fusion), channel_id=1, source_target_pairs={{4,0},{5,1},{6,2},{7,3},{8,4},{9,5},{10,6},{11,7},{12,8},{13,9},{1... | collective-permute-start | bytes 49160 | tf_op jit(solution)/shard_map/ppermute | solution.py:218
  18.4 4.7 %collective-permute-done.2 = f32[32,128]{1,0:T(8,128)S(1)} collective-permute-done((f32[32,128]{1,0:T(8,128)S(1)}, f32[32,128]{1,0:T(8,128)S(1)}, u32[]{:S(2)}, u32[]{:S(2)}) %collective-permute-start.2) | collective-permute-done | bytes 16416 | tf_op jit(solution)/shard_map/ppermute | solution.py:218
  23.1 4.7 %collective-permute-start.3 = (f32[64,128]{1,0:T(8,128)S(1)}, f32[64,128]{1,0:T(8,128)S(1)}, u32[]{:S(2)}, u32[]{:S(2)}) collective-permute-start(f32[64,128]{1,0:T(8,128)S(1)} %concatenate.22), channel_id=1, source_target_pairs={{8,0},{9,1},{10,2},{11,3},{12,4},{13,5},{14,6},{15,7},{0,8},{1,9},... | collective-permute-start | bytes 98312 | tf_op jit(solution)/shard_map/ppermute | solution.py:218
  27.8 3.2 %collective-permute-done.3 = f32[64,128]{1,0:T(8,128)S(1)} collective-permute-done((f32[64,128]{1,0:T(8,128)S(1)}, f32[64,128]{1,0:T(8,128)S(1)}, u32[]{:S(2)}, u32[]{:S(2)}) %collective-permute-start.3) | collective-permute-done | bytes 32800 | tf_op jit(solution)/shard_map/ppermute | solution.py:218
  31.0 0.0 all-to-all-done.gathered_ref
  31.0 1.5 %source.1 = f32[16,136,128]{2,1,0:T(8,128)} custom-call(f32[16,136,128]{2,1,0:T(8,128)S(1)} %all-to-all-done.gathered_ref, f32[128,128]{1,0:T(8,128)S(1)} %concatenate.23.faces_ref), custom_call_target="tpu_custom_call" | custom-call | tf_op jit(solution)/shard_map/source/pallas_call | solution.py:245
  32.5 7.2 %all-to-all-start.1 = ((f32[16,136,128]{2,1,0:T(8,128)}), f32[16,136,128]{2,1,0:T(8,128)S(1)}, u32[]{:S(2)}, u32[]{:S(2)}) async-start(f32[16,136,128]{2,1,0:T(8,128)} %source.1), calls=%async_computation.1 | async-start | bytes 2228224 | tf_op jit(solution)/shard_map/all_to_all | solution.py:254
  39.8 0.9 %slice_reduce_fusion.1 = (f32[512]{0:T(512)S(1)}, f32[512]{0:T(512)S(1)}, f32[512]{0:T(512)S(1)}, f32[512]{0:T(512)S(1)}, f32[512]{0:T(512)S(1)}, /*index=5*/f32[512]{0:T(512)S(1)}, f32[512]{0:T(512)S(1)}, f32[512]{0:T(512)S(1)}) fusion(f32[4,512,128]{2,1,0:T(8,128)S(1)} %bitcast.19), kind=kLoop, calls=%fused_computation.4 | loop fusion | flops 1024 | bytes 32768 | tf_op jit(solution)/shard_map/unstack | solution.py:258
  40.7 0.9 %multiply_reduce_fusion = (f32[4,512]{1,0:T(4,128)S(1)}, f32[4,512]{1,0:T(4,128)S(1)}) fusion(f32[4,512,128]{2,1,0:T(8,128)S(1)} %bitcast.20), kind=kLoop, calls=%fused_computation | loop fusion | flops 4096 | bytes 32768 | tf_op jit(solution)/shard_map/mul | solution.py:260
  41.6 0.6 collective-permute-start.5
  42.3 1.2 %collective-permute-start.4 = (f32[4,512]{1,0:T(4,128)S(1)}, f32[4,512]{1,0:T(4,128)S(1)}, u32[]{:S(2)}, u32[]{:S(2)}) collective-permute-start(f32[4,512]{1,0:T(4,128)S(1)} %fusion.2), channel_id=1, source_target_pairs={{1,0},{2,1},{3,2},{4,3},{5,4},{6,5},{7,6},{8,7},{9,8},{10,9},{11,1... | collective-permute-start | bytes 24584 | tf_op jit(solution)/shard_map/ppermute | solution.py:261
  43.5 1.3 %collective-permute-done.5 = f32[4,512]{1,0:T(4,128)S(1)} collective-permute-done((f32[4,512]{1,0:T(4,128)S(1)}, f32[4,512]{1,0:T(4,128)S(1)}, u32[]{:S(2)}, u32[]{:S(2)}) %collective-permute-start.5) | collective-permute-done | bytes 8224 | tf_op jit(solution)/shard_map/ppermute | solution.py:262
  44.7 1.3 %copy.15.left_ref = f32[4,512,1]{2,1,0:T(8,128)} copy(f32[4,512,1]{1,0,2:T(4,128)S(1)} %bitcast.38) | data formatting | bytes 16384 | tf_op jit(solution)/shard_map/broadcast_in_dim | solution.py:288
  46.1 0.0 collective-permute-done.4
  46.1 1.3 %copy.14.right_ref = f32[4,512,1]{2,1,0:T(8,128)} copy(f32[4,512,1]{1,0,2:T(4,128)S(1)} %bitcast.39) | data formatting | bytes 16384 | tf_op jit(solution)/shard_map/broadcast_in_dim | solution.py:288
  47.4 0.0 copy-start.2
  47.4 1.2 %copy-done.2 = f32[4,512,1]{2,1,0:T(8,128)S(1)} copy-done((f32[4,512,1]{2,1,0:T(8,128)S(1)}, f32[4,512,1]{2,1,0:T(8,128)}, u32[]{:S(2)}) %copy-start.2) | copy-done | bytes 8216
  48.7 0.0 copy-start.3
  48.7 1.2 %copy-done.3 = f32[4,512,1]{2,1,0:T(8,128)S(1)} copy-done((f32[4,512,1]{2,1,0:T(8,128)S(1)}, f32[4,512,1]{2,1,0:T(8,128)}, u32[]{:S(2)}) %copy-start.3) | copy-done | bytes 8216
  49.9 0.0 copy-start.5
  49.9 0.0 copy-start.6
  49.9 3.4 %partial.1.partial_ref = f32[4,512,128]{2,1,0:T(8,128)S(1)} custom-call(f32[4,512,128]{2,1,0:T(8,128)S(1)} %bitcast.21, f32[4,512,128]{2,1,0:T(8,128)S(1)} %bitcast.22, f32[4,512,128]{2,1,0:T(8,128)S(1)} %bitcast.23, f32[4,512,1]{2,1,0:T(8,128)S(1)} %copy-done.3, f32[4,512,1]{2,1,0:T(8,128)S(1)} %copy-done.2), custom_call_target="tpu_custom_call" | custom-call | flops 26214400 | bytes 4194304 | tf_op jit(solution)/shard_map/partial/pallas_call | solution.py:269
  53.3 7.9 %all-to-all-done.1.packed_ref = f32[16,136,128]{2,1,0:T(8,128)S(1)} async-done(((f32[16,136,128]{2,1,0:T(8,128)}), f32[16,136,128]{2,1,0:T(8,128)S(1)}, u32[]{:S(2)}, u32[]{:S(2)}) %all-to-all-start.1) | async-done | bytes 1114144 | tf_op jit(solution)/shard_map/all_to_all | solution.py:254
  61.2 0.0 copy-done.5
  61.2 0.0 copy-done.6
  61.2 1.4 %finish.1 = (f32[4,512,128]{2,1,0:T(8,128)}, f32[4,512,128]{2,1,0:T(8,128)}) custom-call(f32[16,136,128]{2,1,0:T(8,128)S(1)} %all-to-all-done.1.packed_ref, f32[4,512,128]{2,1,0:T(8,128)S(1)} %partial.1.partial_ref, f32[4,512,128]{2,1,0:T(8,128)S(1)} %bitcast.24, s32[4,128]{1,0:T(4,128)S(1)} %bitcast.25, f32[4,128]{1,0:T(4,128)S(1)} %bitcast.26), custom_call_target="tpu_custom_call" | custom-call | tf_op jit(solution)/shard_map/finish/pallas_call | solution.py:289
  (10 shorter events, 0.1 us)
Async XLA Ops:
  0.6 1.2 %copy-start = (f32[1,4,512,128]{3,2,1,0:T(8,128)S(1)}, f32[1,4,512,128]{3,2,1,0:T(8,128)}, u32[]{:S(2)}) copy-start(f32[1,4,512,128]{3,2,1,0:T(8,128)} %param.4) | copy-start | bytes 3145732
  1.9 0.7 %copy-start.4 = (s32[4,1,128]{2,1,0:T(1,128)S(1)}, s32[4,1,128]{2,1,0:T(1,128)}, u32[]{:S(2)}) copy-start(s32[4,1,128]{2,1,0:T(1,128)} %face_ref.1) | copy-start | bytes 6148
  3.6 7.2 %copy-start.1 = (f32[1,4,512,128]{3,2,1,0:T(8,128)S(1)}, f32[1,4,512,128]{3,2,1,0:T(8,128)}, u32[]{:S(2)}) copy-start(f32[1,4,512,128]{3,2,1,0:T(8,128)} %param.4) | copy-start | bytes 3145732
  3.6 27.3 %all-to-all-start = ((f32[16,136,128]{2,1,0:T(8,128)}), f32[16,136,128]{2,1,0:T(8,128)S(1)}, u32[]{:S(2)}, u32[]{:S(2)}) async-start(f32[16,136,128]{2,1,0:T(8,128)} %send.1), calls=%async_computation | async-start | bytes 2228224 | tf_op jit(solution)/shard_map/all_to_all | solution.py:242
  10.9 1.3 %collective-permute-start = (f32[8,128]{1,0:T(8,128)S(1)}, f32[8,128]{1,0:T(8,128)S(1)}, u32[]{:S(2)}, u32[]{:S(2)}) collective-permute-start(f32[8,128]{1,0:T(8,128)S(1)} %pad_maximum_fusion.2), channel_id=1, source_target_pairs={{1,0},{2,1},{3,2},{4,3},{5,4},{6,5},{7,6},{8,7},{9,8},{10,9},{11,1... | collective-permute-start | bytes 12296 | tf_op jit(solution)/shard_map/ppermute | solution.py:218
  12.2 4.9 %collective-permute-start.1 = (f32[16,128]{1,0:T(8,128)S(1)}, f32[16,128]{1,0:T(8,128)S(1)}, u32[]{:S(2)}, u32[]{:S(2)}) collective-permute-start(f32[16,128]{1,0:T(8,128)S(1)} %pad_maximum_fusion.1), channel_id=1, source_target_pairs={{2,0},{3,1},{4,2},{5,3},{6,4},{7,5},{8,6},{9,7},{10,8},{11,9},{12,... | collective-permute-start | bytes 24584 | tf_op jit(solution)/shard_map/ppermute | solution.py:218
  17.1 5.9 %collective-permute-start.2 = (f32[32,128]{1,0:T(8,128)S(1)}, f32[32,128]{1,0:T(8,128)S(1)}, u32[]{:S(2)}, u32[]{:S(2)}) collective-permute-start(f32[32,128]{1,0:T(8,128)S(1)} %pad_maximum_fusion), channel_id=1, source_target_pairs={{4,0},{5,1},{6,2},{7,3},{8,4},{9,5},{10,6},{11,7},{12,8},{13,9},{1... | collective-permute-start | bytes 49160 | tf_op jit(solution)/shard_map/ppermute | solution.py:218
  23.1 7.9 %collective-permute-start.3 = (f32[64,128]{1,0:T(8,128)S(1)}, f32[64,128]{1,0:T(8,128)S(1)}, u32[]{:S(2)}, u32[]{:S(2)}) collective-permute-start(f32[64,128]{1,0:T(8,128)S(1)} %concatenate.22), channel_id=1, source_target_pairs={{8,0},{9,1},{10,2},{11,3},{12,4},{13,5},{14,6},{15,7},{0,8},{1,9},... | collective-permute-start | bytes 98312 | tf_op jit(solution)/shard_map/ppermute | solution.py:218
  32.5 28.7 %all-to-all-start.1 = ((f32[16,136,128]{2,1,0:T(8,128)}), f32[16,136,128]{2,1,0:T(8,128)S(1)}, u32[]{:S(2)}, u32[]{:S(2)}) async-start(f32[16,136,128]{2,1,0:T(8,128)} %source.1), calls=%async_computation.1 | async-start | bytes 2228224 | tf_op jit(solution)/shard_map/all_to_all | solution.py:254
  41.6 3.1 %collective-permute-start.5 = (f32[4,512]{1,0:T(4,128)S(1)}, f32[4,512]{1,0:T(4,128)S(1)}, u32[]{:S(2)}, u32[]{:S(2)}) collective-permute-start(f32[4,512]{1,0:T(4,128)S(1)} %fusion.3), channel_id=1, source_target_pairs={{0,1},{1,2},{2,3},{3,4},{4,5},{5,6},{6,7},{7,8},{8,9},{9,10},{10,1... | collective-permute-start | bytes 24584 | tf_op jit(solution)/shard_map/ppermute | solution.py:262
  42.3 3.8 %collective-permute-start.4 = (f32[4,512]{1,0:T(4,128)S(1)}, f32[4,512]{1,0:T(4,128)S(1)}, u32[]{:S(2)}, u32[]{:S(2)}) collective-permute-start(f32[4,512]{1,0:T(4,128)S(1)} %fusion.2), channel_id=1, source_target_pairs={{1,0},{2,1},{3,2},{4,3},{5,4},{6,5},{7,6},{8,7},{9,8},{10,9},{11,1... | collective-permute-start | bytes 24584 | tf_op jit(solution)/shard_map/ppermute | solution.py:261
  47.4 1.2 %copy-start.2 = (f32[4,512,1]{2,1,0:T(8,128)S(1)}, f32[4,512,1]{2,1,0:T(8,128)}, u32[]{:S(2)}) copy-start(f32[4,512,1]{2,1,0:T(8,128)} %copy.15.left_ref) | copy-start | bytes 24580
  48.7 1.2 %copy-start.3 = (f32[4,512,1]{2,1,0:T(8,128)S(1)}, f32[4,512,1]{2,1,0:T(8,128)}, u32[]{:S(2)}) copy-start(f32[4,512,1]{2,1,0:T(8,128)} %copy.14.right_ref) | copy-start | bytes 24580
  49.9 11.4 %copy-start.5 = (s32[4,1,128]{2,1,0:T(1,128)S(1)}, s32[4,1,128]{2,1,0:T(1,128)}, u32[]{:S(2)}) copy-start(s32[4,1,128]{2,1,0:T(1,128)} %param.5) | copy-start | bytes 6148
  49.9 11.4 %copy-start.6 = (f32[4,1,128]{2,1,0:T(1,128)S(1)}, f32[4,1,128]{2,1,0:T(1,128)}, u32[]{:S(2)}) copy-start(f32[4,1,128]{2,1,0:T(1,128)} %param.7) | copy-start | bytes 6148

commit v3 on v2

--- a/solution.py
+++ b/solution.py
@@ -16,6 +16,7 @@
 PSEUDO_STEP = 0.2
 LANES = 128
 ROWS = 8
+PIECES = 4
 
 
 def pitch_coefficients(count, omega):
@@ -36,12 +37,17 @@
     return outs
 
 
-def send_kernel(cells_ref, face_ref, out_ref, want_ref, sems):
-    depth = out_ref.shape[1] - ROWS
+def send_kernel(cells_ref, face_ref, out_ref, held_ref, want_ref, sems):
+    count, depth = out_ref.shape[0], out_ref.shape[1] - ROWS
+    group = count // PIECES
     asked = pltpu.make_async_copy(face_ref, want_ref, sems.at[0])
     asked.start()
-    chunks = pltpu.make_async_copy(cells_ref, out_ref.at[:, pl.ds(0, depth), :], sems.at[1])
-    chunks.start()
+    arrivals = []
+    for p in range(PIECES):
+        part = pl.ds(p * group, group)
+        copy = pltpu.make_async_copy(cells_ref.at[part], held_ref.at[part, pl.ds(0, depth), :], sems.at[1 + p])
+        copy.start()
+        arrivals.append(copy)
     asked.wait()
     lower = lax.broadcasted_iota(jnp.int32, (ROWS, LANES), 0) < 4
     want = jnp.where(
@@ -49,40 +55,56 @@
         jnp.broadcast_to(want_ref[0], (ROWS, LANES)),
         jnp.broadcast_to(want_ref[1], (ROWS, LANES)),
     ).astype(jnp.float32)
-    for j in range(out_ref.shape[0]):
-        out_ref[j, depth : depth + ROWS, :] = want
-    chunks.wait()
-
-
-def source_kernel(gathered_ref, faces_ref, out_ref):
+    for j in range(count):
+        held_ref[j, depth : depth + ROWS, :] = want
+    leaving = []
+    for p in range(PIECES):
+        part = pl.ds(p * group, group)
+        arrivals[p].wait()
+        copy = pltpu.make_async_copy(held_ref.at[part], out_ref.at[part], sems.at[1 + PIECES + p])
+        copy.start()
+        leaving.append(copy)
+    for copy in leaving:
+        copy.wait()
+
+
+def source_kernel(gathered_ref, faces_ref, out_ref, held_ref, sems):
     depth = gathered_ref.shape[1] - ROWS
     slab = lax.axis_index("cell")
-
-    def strip(t, carry):
-        rows = pl.ds(pl.multiple_of(t * ROWS, ROWS), ROWS)
-        values = [gathered_ref[i, rows, :] for i in range(INST)]
-        outs = coupled(values[:ROTOR_INST], OMEGA_ROTOR) + coupled(values[ROTOR_INST:], OMEGA_STATOR)
-        for i in range(INST):
-            out_ref[i, rows, :] = outs[i]
-        return carry
-
-    lax.fori_loop(0, depth // ROWS, strip, 0, unroll=2)
-
     slabs = faces_ref.shape[0] // ROWS
+    span = depth // PIECES
+    leaving = []
+
+    def leave(k, first, size):
+        part = pl.ds(first, size)
+        copy = pltpu.make_async_copy(held_ref.at[:, part, :], out_ref.at[:, part, :], sems.at[k])
+        copy.start()
+        leaving.append(copy)
+
+    def tile(ahead):
+        place = (ahead & 3) * (slabs // 4) + (ahead >> 2)
+        return faces_ref[pl.ds(pl.multiple_of(place * ROWS, ROWS), ROWS), :]
+
     wants = [gathered_ref[i, depth : depth + ROWS, :].astype(jnp.int32) for i in range(INST)]
-    firsts = [(want[0, 0] >> 7) & (slabs - 1) for want in wants]
-    windows = []
-    for want, first in zip(wants, firsts):
+    firsts = [want[0, 0] >> 7 for want in wants]
+
+    for p in range(PIECES):
+        for t in range(p * span, (p + 1) * span, ROWS):
+            values = [gathered_ref[i, t : t + ROWS, :] for i in range(INST)]
+            outs = coupled(values[:ROTOR_INST], OMEGA_ROTOR) + coupled(values[ROTOR_INST:], OMEGA_STATOR)
+            for i in range(INST):
+                held_ref[i, t : t + ROWS, :] = outs[i]
+        if p < PIECES - 1:
+            leave(p, p * span, span)
+    for i, (want, first) in enumerate(zip(wants, firsts)):
         ahead = (first - slab) & (slabs - 1)
-        here = faces_ref[pl.ds(pl.multiple_of(ahead * ROWS, ROWS), ROWS), :]
-        ahead = (ahead + 1) & (slabs - 1)
-        after = faces_ref[pl.ds(pl.multiple_of(ahead * ROWS, ROWS), ROWS), :]
         place = want & (LANES - 1)
-        here = jnp.take_along_axis(here, place, axis=1, mode="promise_in_bounds")
-        after = jnp.take_along_axis(after, place, axis=1, mode="promise_in_bounds")
-        windows.append(jnp.where((want >> 7) == first, here, after))
-    for i in range(INST):
-        out_ref[i, depth : depth + ROWS, :] = windows[i]
+        here = jnp.take_along_axis(tile(ahead), place, axis=1, mode="promise_in_bounds")
+        after = jnp.take_along_axis(tile((ahead + 1) & (slabs - 1)), place, axis=1, mode="promise_in_bounds")
+        held_ref[i, depth : depth + ROWS, :] = jnp.where((want >> 7) == first, here, after)
+    leave(PIECES - 1, depth - span, span + ROWS)
+    for copy in leaving:
+        copy.wait()
 
 
 def fluxes(r, m, n, e):
@@ -97,8 +119,31 @@
     return (m, ma + p, mb, h * a), (n, mb, nb + p, h * b)
 
 
+def edge_kernel(cells_ref, export_ref, head_ref, tail_ref):
+    axial = cells_ref.shape[1]
+    rotor = lax.axis_index("inst") < ROTOR_INST
+    for c in range(4):
+        row = jnp.where(rotor, cells_ref[c, axial - 1 : axial, :], cells_ref[c, 0:1, :])
+        export_ref[c : c + 1, :] = row
+        export_ref[4 + c : 5 + c, :] = row
+    lane = lax.broadcasted_iota(jnp.int32, (LANES, LANES), 1)
+    for first in range(0, axial, LANES):
+        span = pl.ds(first, LANES)
+        sides = jnp.zeros((LANES, LANES), jnp.float32)
+        for c in range(4):
+            u = cells_ref[c, span, :]
+            sides = jnp.where(lane == c, pltpu.roll(u, c, 1) if c else u, sides)
+            sides = jnp.where(lane == 4 + c, pltpu.roll(u, 5 + c, 1), sides)
+        sides = sides.T
+        for ref, at, sign in ((head_ref, 0, -1.0), (tail_ref, 4, 1.0)):
+            u = [sides[at + c : at + c + 1, :] for c in range(4)]
+            _, flux_y = fluxes(*u)
+            for c in range(4):
+                ref[c : c + 1, span] = 0.5 * flux_y[c] + sign * DAMPING_COEF * u[c]
+
+
 def partial_kernel(
-    cur_ref, prev_ref, next_ref, right_ref, left_ref, out_ref, plus_ref, minus_ref
+    cur_ref, prev_ref, next_ref, right_ref, left_ref, out_ref, plus_ref, minus_ref, side_ref
 ):
     block = pl.program_id(0)
     last = pl.num_programs(0) - 1
@@ -123,20 +168,23 @@
         )
 
     lane = lax.broadcasted_iota(jnp.int32, (ROWS, LANES), 1)
+    sides = jnp.concatenate([right_ref[...], left_ref[...], jnp.zeros((LANES - 8, LANES), jnp.float32)], 0)
+    side_ref[...] = sides.T
 
     def first(t, carry):
         rows = pl.ds(pl.multiple_of(t * ROWS, ROWS), ROWS)
         shifted = pl.ds(pl.multiple_of(t * ROWS + ROWS, ROWS), ROWS)
         u = [cur_ref[c, rows, :] for c in range(4)]
         flux_x, flux_y = fluxes(*u)
+        side = side_ref[rows, :]
         for c in range(4):
             half_x = 0.5 * flux_x[c]
             half_y = 0.5 * flux_y[c]
             damped = DAMPING_COEF * u[c]
             plus_ref[c, shifted, :] = half_x - damped
             minus_ref[c, shifted, :] = half_x + damped
-            up = jnp.where(lane == 0, right_ref[c, rows, :], half_y - damped)
-            down = jnp.where(lane == LANES - 1, left_ref[c, rows, :], half_y + damped)
+            up = jnp.where(lane == 0, jnp.broadcast_to(side[:, c : c + 1], (ROWS, LANES)), half_y - damped)
+            down = jnp.where(lane == LANES - 1, jnp.broadcast_to(side[:, 4 + c : 5 + c], (ROWS, LANES)), half_y + damped)
             out_ref[c, rows, :] = (
                 pltpu.roll(up, LANES - 1, 1) - pltpu.roll(down, 1, 1) + (4.0 * DAMPING_COEF) * u[c]
             )
@@ -212,11 +260,12 @@
 
 def collected(block, axis):
     count = lax.axis_size(axis)
-    step = 1
-    while step < count:
-        pairs = [((i + step) % count, i) for i in range(count)]
-        block = jnp.concatenate([block, lax.ppermute(block, axis, pairs)], 0)
-        step *= 2
+    for step in (count // 4, 1):
+        blocks = [block]
+        for k in range(1, 4):
+            pairs = [((i + k * step) % count, i) for i in range(count)]
+            blocks.append(lax.ppermute(block, axis, pairs))
+        block = jnp.concatenate(blocks, 0)
     return block
 
 
@@ -225,39 +274,54 @@
     axial, width = cells.shape[1], cells.shape[2]
     inst_count = lax.axis_size("inst")
     cell_count = lax.axis_size("cell")
-    rotor = lax.axis_index("inst") < ROTOR_INST
     depth = 4 * axial // inst_count
 
     vmem = pl.BlockSpec(memory_space=pltpu.VMEM)
     anywhere = pl.BlockSpec(memory_space=pl.ANY)
     sent = pl.pallas_call(
         send_kernel,
-        out_shape=pltpu.VMEM((inst_count, depth + ROWS, width), jnp.float32),
+        out_shape=jax.ShapeDtypeStruct((inst_count, depth + ROWS, width), jnp.float32),
         in_specs=[anywhere, anywhere],
-        out_specs=vmem,
-        scratch_shapes=[pltpu.VMEM(src_face.shape, jnp.int32), pltpu.SemaphoreType.DMA((2,))],
-        compiler_params=pltpu.CompilerParams(vmem_limit_bytes=16 << 20),
+        out_specs=anywhere,
+        scratch_shapes=[
+            pltpu.VMEM((inst_count, depth + ROWS, width), jnp.float32),
+            pltpu.VMEM(src_face.shape, jnp.int32),
+            pltpu.SemaphoreType.DMA((1 + 2 * PIECES,)),
+        ],
+        compiler_params=pltpu.CompilerParams(vmem_limit_bytes=60 << 20),
         name="send",
     )(cells.reshape(inst_count, depth, width), src_face)
+    sent, cells = lax.optimization_barrier((sent, cells))
+    export, head, tail = pl.pallas_call(
+        edge_kernel,
+        out_shape=[
+            jax.ShapeDtypeStruct((ROWS, width), jnp.float32),
+            jax.ShapeDtypeStruct((4, axial), jnp.float32),
+            jax.ShapeDtypeStruct((4, axial), jnp.float32),
+        ],
+        in_specs=[vmem],
+        out_specs=[vmem] * 3,
+        compiler_params=pltpu.CompilerParams(vmem_limit_bytes=16 << 20),
+        cost_estimate=pl.CostEstimate(flops=0, bytes_accessed=32 << 20, transcendentals=0),
+        name="edges",
+    )(cells)
     gathered = lax.all_to_all(sent, "inst", 0, 0)
-    export = jnp.where(rotor, cells[:, -1, :], cells[:, 0, :])
-    faces = collected(jnp.concatenate([export, export], 0), "cell")
+    faces = collected(export, "cell")
     packed = pl.pallas_call(
         source_kernel,
-        out_shape=pltpu.VMEM((inst_count, depth + ROWS, width), jnp.float32),
+        out_shape=jax.ShapeDtypeStruct((inst_count, depth + ROWS, width), jnp.float32),
         in_specs=[vmem, vmem],
-        out_specs=vmem,
+        out_specs=anywhere,
+        scratch_shapes=[
+            pltpu.VMEM((inst_count, depth + ROWS, width), jnp.float32),
+            pltpu.SemaphoreType.DMA((PIECES,)),
+        ],
         compiler_params=pltpu.CompilerParams(vmem_limit_bytes=16 << 20),
         name="source",
     )(gathered, faces)
-    cells, packed = lax.optimization_barrier((cells, packed))
+    head, tail, packed = lax.optimization_barrier((head, tail, packed))
     packed = lax.all_to_all(packed, "inst", 0, 0)
 
-    head, tail = cells[:, :, 0], cells[:, :, width - 1]
-    _, head_flux = fluxes(*head)
-    _, tail_flux = fluxes(*tail)
-    head = 0.5 * jnp.stack(head_flux) - DAMPING_COEF * head
-    tail = 0.5 * jnp.stack(tail_flux) + DAMPING_COEF * tail
     right = lax.ppermute(head, "cell", [((i + 1) % cell_count, i) for i in range(cell_count)])
     left = lax.ppermute(tail, "cell", [(i, (i + 1) % cell_count) for i in range(cell_count)])
 
@@ -265,7 +329,7 @@
     per = depth // ROWS
     strips = axial // ROWS
     block_spec = pl.BlockSpec((4, depth, width), lambda g: (0, g, 0))
-    halo_spec = pl.BlockSpec((4, depth, 1), lambda g: (0, g, 0))
+    halo_spec = pl.BlockSpec((4, depth), lambda g: (0, g))
     partial = pl.pallas_call(
         partial_kernel,
         grid=(blocks,),
@@ -281,11 +345,12 @@
         scratch_shapes=[
             pltpu.VMEM((4, depth + 2 * ROWS, width), jnp.float32),
             pltpu.VMEM((4, depth + 2 * ROWS, width), jnp.float32),
+            pltpu.VMEM((depth, width), jnp.float32),
         ],
         compiler_params=pltpu.CompilerParams(vmem_limit_bytes=16 << 20),
         cost_estimate=pl.CostEstimate(flops=100 * cells.size, bytes_accessed=16 * cells.size, transcendentals=0),
         name="partial",
-    )(cells, cells, cells, right[:, :, None], left[:, :, None])
+    )(cells, cells, cells, right, left)
     residual, new_state = pl.pallas_call(
         finish_kernel,
         out_shape=[jax.ShapeDtypeStruct(cells.shape, jnp.float32)] * 2,

time: 63.1 us -> 57.9 us (0.918)
  the two profiles are of different devices: /device:TPU:96 before, /device:TPU:64 now
where the time goes in v3:
time: 57.9 us; the launch traced here: 57 us
  starting transfers between devices  27.7 us (48%)
  waiting for transfers between devices  19.1 us (33%)
  Pallas kernels  9.43 us (16%)
  between operations  0.73 us (1%)
    ppermute x6, starting transfers between devices, collected(): blocks.append(lax.ppermute(block, axis, pairs))  12.8 us
    all_to_all x1, waiting for transfers between devices, on_device(): packed = lax.all_to_all(packed, 'inst', 0, 0)  10.7 us
    all_to_all x1, starting transfers between devices, on_device(): packed = lax.all_to_all(packed, 'inst', 0, 0)  7.23 us
    all_to_all x1, starting transfers between devices, on_device(): gathered = lax.all_to_all(sent, 'inst', 0, 0)  7.18 us
    ppermute x6, waiting for transfers between devices, collected(): blocks.append(lax.ppermute(block, axis, pairs))  5.12 us
    pallas_call x1, Pallas kernels, on_device(): pl.pallas_call(partial_kernel, grid=(blocks,), out_shape=pltpu.VMEM(cells...  4.03 us
    ppermute x1, waiting for transfers between devices, on_device(): lax.ppermute(tail, 'cell', [(i, (i + 1) % cell_count) for i in range(cell...  2.38 us
    pallas_call x1, Pallas kernels, on_device(): pl.pallas_call(send_kernel, out_shape=jax.ShapeDtypeStruct((inst_count, d...  2.05 us
  transfers between devices with their start and end apart: 10, of which 6 were waited for; matrix products, arithmetic and copies ran while one was open for 0% of the time, Pallas kernels for 8%

profile of v3, /device:TPU:64, one launch (start us, length us, event | category | flops | bytes accessed | tf_op | source)
XLA Modules:
  0.0 57.0 jit_solution(10485760914583780372)
XLA Ops:
  0.6 2.1 %send.1 = f32[16,136,128]{2,1,0:T(8,128)} custom-call(f32[16,128,128]{2,1,0:T(8,128)} %bitcast.6, s32[4,1,128]{2,1,0:T(1,128)} %face_ref.1), custom_call_target="tpu_custom_call" | custom-call | tf_op jit(solution)/shard_map/send/pallas_call | solution.py:281
  2.7 0.0 copy-start
  2.7 7.2 %all-to-all-start = ((f32[16,136,128]{2,1,0:T(8,128)}), f32[16,136,128]{2,1,0:T(8,128)S(1)}, u32[]{:S(2)}, u32[]{:S(2)}) async-start(f32[16,136,128]{2,1,0:T(8,128)} %send.1), calls=%async_computation | async-start | bytes 2228224 | tf_op jit(solution)/shard_map/all_to_all | solution.py:308
  9.9 0.0 copy-done
  9.9 0.7 %edges.1 = (f32[8,128]{1,0:T(8,128)S(1)}, f32[4,512]{1,0:T(4,128)S(1)}, f32[4,512]{1,0:T(4,128)S(1)}) custom-call(f32[4,512,128]{2,1,0:T(8,128)S(1)} %bitcast.7), custom_call_target="tpu_custom_call" | custom-call | bytes 33554432 | tf_op jit(solution)/shard_map/edges/pallas_call | solution.py:295
  10.6 4.6 %collective-permute-start.2 = (f32[8,128]{1,0:T(8,128)S(1)}, f32[8,128]{1,0:T(8,128)S(1)}, u32[]{:S(2)}, u32[]{:S(2)}) collective-permute-start(f32[8,128]{1,0:T(8,128)S(1)} %get-tuple-element.16), channel_id=1, source_target_pairs={{12,0},{13,1},{14,2},{15,3},{0,4},{1,5},{2,6},{3,7},{4,8},{5,9},{6... | collective-permute-start | bytes 12296 | tf_op jit(solution)/shard_map/ppermute | solution.py:267
  15.2 1.0 %collective-permute-start.1 = (f32[8,128]{1,0:T(8,128)S(1)}, f32[8,128]{1,0:T(8,128)S(1)}, u32[]{:S(2)}, u32[]{:S(2)}) collective-permute-start(f32[8,128]{1,0:T(8,128)S(1)} %get-tuple-element.16), channel_id=1, source_target_pairs={{8,0},{9,1},{10,2},{11,3},{12,4},{13,5},{14,6},{15,7},{0,8},{1,9},... | collective-permute-start | bytes 12296 | tf_op jit(solution)/shard_map/ppermute | solution.py:267
  16.2 2.8 %collective-permute-start = (f32[8,128]{1,0:T(8,128)S(1)}, f32[8,128]{1,0:T(8,128)S(1)}, u32[]{:S(2)}, u32[]{:S(2)}) collective-permute-start(f32[8,128]{1,0:T(8,128)S(1)} %get-tuple-element.16), channel_id=1, source_target_pairs={{4,0},{5,1},{6,2},{7,3},{8,4},{9,5},{10,6},{11,7},{12,8},{13,9},{1... | collective-permute-start | bytes 12296 | tf_op jit(solution)/shard_map/ppermute | solution.py:267
  19.0 2.9 %collective-permute-done = f32[8,128]{1,0:T(8,128)S(1)} collective-permute-done((f32[8,128]{1,0:T(8,128)S(1)}, f32[8,128]{1,0:T(8,128)S(1)}, u32[]{:S(2)}, u32[]{:S(2)}) %collective-permute-start) | collective-permute-done | bytes 4128 | tf_op jit(solution)/shard_map/ppermute | solution.py:267
  21.9 0.8 %collective-permute-done.1 = f32[8,128]{1,0:T(8,128)S(1)} collective-permute-done((f32[8,128]{1,0:T(8,128)S(1)}, f32[8,128]{1,0:T(8,128)S(1)}, u32[]{:S(2)}, u32[]{:S(2)}) %collective-permute-start.1) | collective-permute-done | bytes 4128 | tf_op jit(solution)/shard_map/ppermute | solution.py:267
  22.7 0.0 collective-permute-done.2
  22.7 0.0 collective-permute-start.3
  22.7 0.9 %collective-permute-start.5 = (f32[32,128]{1,0:T(8,128)S(1)}, f32[32,128]{1,0:T(8,128)S(1)}, u32[]{:S(2)}, u32[]{:S(2)}) collective-permute-start(f32[32,128]{1,0:T(8,128)S(1)} %get-tuple-element.22), channel_id=1, source_target_pairs={{3,0},{4,1},{5,2},{6,3},{7,4},{8,5},{9,6},{10,7},{11,8},{12,9},{13... | collective-permute-start | bytes 49160 | tf_op jit(solution)/shard_map/ppermute | solution.py:267
  23.6 3.4 %collective-permute-start.4 = (f32[32,128]{1,0:T(8,128)S(1)}, f32[32,128]{1,0:T(8,128)S(1)}, u32[]{:S(2)}, u32[]{:S(2)}) collective-permute-start(f32[32,128]{1,0:T(8,128)S(1)} %get-tuple-element.22), channel_id=1, source_target_pairs={{2,0},{3,1},{4,2},{5,3},{6,4},{7,5},{8,6},{9,7},{10,8},{11,9},{12,... | collective-permute-start | bytes 49160 | tf_op jit(solution)/shard_map/ppermute | solution.py:267
  27.1 0.0 collective-permute-done.3
  27.1 1.4 %collective-permute-done.4 = f32[32,128]{1,0:T(8,128)S(1)} collective-permute-done((f32[32,128]{1,0:T(8,128)S(1)}, f32[32,128]{1,0:T(8,128)S(1)}, u32[]{:S(2)}, u32[]{:S(2)}) %collective-permute-start.4) | collective-permute-done | bytes 16416 | tf_op jit(solution)/shard_map/ppermute | solution.py:267
  28.5 0.0 collective-permute-done.5
  28.5 0.0 all-to-all-done.gathered_ref
  28.5 1.2 %source.1 = f32[16,136,128]{2,1,0:T(8,128)} custom-call(f32[16,136,128]{2,1,0:T(8,128)S(1)} %all-to-all-done.gathered_ref, f32[128,128]{1,0:T(8,128)S(1)} %constant_dynamic-update-slice_fusion.4.faces_ref), custom_call_target="tpu_custom_call" | custom-call | tf_op jit(solution)/shard_map/source/pallas_call | solution.py:310
  29.8 7.2 %all-to-all-start.1 = ((f32[16,136,128]{2,1,0:T(8,128)}), f32[16,136,128]{2,1,0:T(8,128)S(1)}, u32[]{:S(2)}, u32[]{:S(2)}) async-start(f32[16,136,128]{2,1,0:T(8,128)} %source.1), calls=%async_computation.1 | async-start | bytes 2228224 | tf_op jit(solution)/shard_map/all_to_all | solution.py:323
  37.0 0.0 copy-start.1
  37.0 0.0 copy-start.2
  37.0 0.0 collective-permute-start.6
  37.0 0.5 collective-permute-start.7
  37.5 0.9 %collective-permute-done.6.right_ref = f32[4,512]{1,0:T(4,128)S(1)} collective-permute-done((f32[4,512]{1,0:T(4,128)S(1)}, f32[4,512]{1,0:T(4,128)S(1)}, u32[]{:S(2)}, u32[]{:S(2)}) %collective-permute-start.6) | collective-permute-done | bytes 8224 | tf_op jit(solution)/shard_map/ppermute | solution.py:325
  38.4 2.4 %collective-permute-done.7.left_ref = f32[4,512]{1,0:T(4,128)S(1)} collective-permute-done((f32[4,512]{1,0:T(4,128)S(1)}, f32[4,512]{1,0:T(4,128)S(1)}, u32[]{:S(2)}, u32[]{:S(2)}) %collective-permute-start.7) | collective-permute-done | bytes 8224 | tf_op jit(solution)/shard_map/ppermute | solution.py:326
  40.8 4.0 %partial.1.partial_ref = f32[4,512,128]{2,1,0:T(8,128)S(1)} custom-call(f32[4,512,128]{2,1,0:T(8,128)S(1)} %bitcast.8, f32[4,512,128]{2,1,0:T(8,128)S(1)} %bitcast.9, f32[4,512,128]{2,1,0:T(8,128)S(1)} %bitcast.10, f32[4,512]{1,0:T(4,128)S(1)} %collective-permute-done.6.right_ref, f32[4,512]{1,0:T(4,128)S(1)} %collective-permute-done.7.left_ref), custom_call_target="tpu_custom_call" | custom-call | flops 26214400 | bytes 4194304 | tf_op jit(solution)/shard_map/partial/pallas_call | solution.py:333
  44.8 10.7 %all-to-all-done.1.packed_ref = f32[16,136,128]{2,1,0:T(8,128)S(1)} async-done(((f32[16,136,128]{2,1,0:T(8,128)}), f32[16,136,128]{2,1,0:T(8,128)S(1)}, u32[]{:S(2)}, u32[]{:S(2)}) %all-to-all-start.1) | async-done | bytes 1114144 | tf_op jit(solution)/shard_map/all_to_all | solution.py:323
  55.5 0.0 copy-done.1
  55.5 0.0 copy-done.2
  55.5 1.4 %finish.1 = (f32[4,512,128]{2,1,0:T(8,128)}, f32[4,512,128]{2,1,0:T(8,128)}) custom-call(f32[16,136,128]{2,1,0:T(8,128)S(1)} %all-to-all-done.1.packed_ref, f32[4,512,128]{2,1,0:T(8,128)S(1)} %partial.1.partial_ref, f32[4,512,128]{2,1,0:T(8,128)S(1)} %bitcast.11, s32[4,128]{1,0:T(4,128)S(1)} %bitcast.12, f32[4,128]{1,0:T(4,128)S(1)} %bitcast.13), custom_call_target="tpu_custom_call" | custom-call | tf_op jit(solution)/shard_map/finish/pallas_call | solution.py:354
  (7 shorter events, 0.0 us)
Async XLA Ops:
  2.7 7.2 %copy-start = (f32[1,4,512,128]{3,2,1,0:T(8,128)S(1)}, f32[1,4,512,128]{3,2,1,0:T(8,128)}, u32[]{:S(2)}) copy-start(f32[1,4,512,128]{3,2,1,0:T(8,128)} %param.4) | copy-start | bytes 3145732
  2.7 25.8 %all-to-all-start = ((f32[16,136,128]{2,1,0:T(8,128)}), f32[16,136,128]{2,1,0:T(8,128)S(1)}, u32[]{:S(2)}, u32[]{:S(2)}) async-start(f32[16,136,128]{2,1,0:T(8,128)} %send.1), calls=%async_computation | async-start | bytes 2228224 | tf_op jit(solution)/shard_map/all_to_all | solution.py:308
  10.6 12.1 %collective-permute-start.2 = (f32[8,128]{1,0:T(8,128)S(1)}, f32[8,128]{1,0:T(8,128)S(1)}, u32[]{:S(2)}, u32[]{:S(2)}) collective-permute-start(f32[8,128]{1,0:T(8,128)S(1)} %get-tuple-element.16), channel_id=1, source_target_pairs={{12,0},{13,1},{14,2},{15,3},{0,4},{1,5},{2,6},{3,7},{4,8},{5,9},{6... | collective-permute-start | bytes 12296 | tf_op jit(solution)/shard_map/ppermute | solution.py:267
  15.2 7.5 %collective-permute-start.1 = (f32[8,128]{1,0:T(8,128)S(1)}, f32[8,128]{1,0:T(8,128)S(1)}, u32[]{:S(2)}, u32[]{:S(2)}) collective-permute-start(f32[8,128]{1,0:T(8,128)S(1)} %get-tuple-element.16), channel_id=1, source_target_pairs={{8,0},{9,1},{10,2},{11,3},{12,4},{13,5},{14,6},{15,7},{0,8},{1,9},... | collective-permute-start | bytes 12296 | tf_op jit(solution)/shard_map/ppermute | solution.py:267
  16.2 5.7 %collective-permute-start = (f32[8,128]{1,0:T(8,128)S(1)}, f32[8,128]{1,0:T(8,128)S(1)}, u32[]{:S(2)}, u32[]{:S(2)}) collective-permute-start(f32[8,128]{1,0:T(8,128)S(1)} %get-tuple-element.16), channel_id=1, source_target_pairs={{4,0},{5,1},{6,2},{7,3},{8,4},{9,5},{10,6},{11,7},{12,8},{13,9},{1... | collective-permute-start | bytes 12296 | tf_op jit(solution)/shard_map/ppermute | solution.py:267
  22.7 4.4 %collective-permute-start.3 = (f32[32,128]{1,0:T(8,128)S(1)}, f32[32,128]{1,0:T(8,128)S(1)}, u32[]{:S(2)}, u32[]{:S(2)}) collective-permute-start(f32[32,128]{1,0:T(8,128)S(1)} %get-tuple-element.22), channel_id=1, source_target_pairs={{1,0},{2,1},{3,2},{4,3},{5,4},{6,5},{7,6},{8,7},{9,8},{10,9},{11,1... | collective-permute-start | bytes 49160 | tf_op jit(solution)/shard_map/ppermute | solution.py:267
  22.7 5.8 %collective-permute-start.5 = (f32[32,128]{1,0:T(8,128)S(1)}, f32[32,128]{1,0:T(8,128)S(1)}, u32[]{:S(2)}, u32[]{:S(2)}) collective-permute-start(f32[32,128]{1,0:T(8,128)S(1)} %get-tuple-element.22), channel_id=1, source_target_pairs={{3,0},{4,1},{5,2},{6,3},{7,4},{8,5},{9,6},{10,7},{11,8},{12,9},{13... | collective-permute-start | bytes 49160 | tf_op jit(solution)/shard_map/ppermute | solution.py:267
  23.6 4.9 %collective-permute-start.4 = (f32[32,128]{1,0:T(8,128)S(1)}, f32[32,128]{1,0:T(8,128)S(1)}, u32[]{:S(2)}, u32[]{:S(2)}) collective-permute-start(f32[32,128]{1,0:T(8,128)S(1)} %get-tuple-element.22), channel_id=1, source_target_pairs={{2,0},{3,1},{4,2},{5,3},{6,4},{7,5},{8,6},{9,7},{10,8},{11,9},{12,... | collective-permute-start | bytes 49160 | tf_op jit(solution)/shard_map/ppermute | solution.py:267
  29.8 25.8 %all-to-all-start.1 = ((f32[16,136,128]{2,1,0:T(8,128)}), f32[16,136,128]{2,1,0:T(8,128)S(1)}, u32[]{:S(2)}, u32[]{:S(2)}) async-start(f32[16,136,128]{2,1,0:T(8,128)} %source.1), calls=%async_computation.1 | async-start | bytes 2228224 | tf_op jit(solution)/shard_map/all_to_all | solution.py:323
  37.0 18.5 %copy-start.1 = (s32[4,1,128]{2,1,0:T(1,128)S(1)}, s32[4,1,128]{2,1,0:T(1,128)}, u32[]{:S(2)}) copy-start(s32[4,1,128]{2,1,0:T(1,128)} %param.5) | copy-start | bytes 6148
  37.0 18.5 %copy-start.2 = (f32[4,1,128]{2,1,0:T(1,128)S(1)}, f32[4,1,128]{2,1,0:T(1,128)}, u32[]{:S(2)}) copy-start(f32[4,1,128]{2,1,0:T(1,128)} %param.7) | copy-start | bytes 6148
  37.0 1.4 %collective-permute-start.6 = (f32[4,512]{1,0:T(4,128)S(1)}, f32[4,512]{1,0:T(4,128)S(1)}, u32[]{:S(2)}, u32[]{:S(2)}) collective-permute-start(f32[4,512]{1,0:T(4,128)S(1)} %get-tuple-element.18), channel_id=1, source_target_pairs={{1,0},{2,1},{3,2},{4,3},{5,4},{6,5},{7,6},{8,7},{9,8},{10,9},{11,1... | collective-permute-start | bytes 24584 | tf_op jit(solution)/shard_map/ppermute | solution.py:325
  37.0 3.7 %collective-permute-start.7 = (f32[4,512]{1,0:T(4,128)S(1)}, f32[4,512]{1,0:T(4,128)S(1)}, u32[]{:S(2)}, u32[]{:S(2)}) collective-permute-start(f32[4,512]{1,0:T(4,128)S(1)} %get-tuple-element.19), channel_id=1, source_target_pairs={{0,1},{1,2},{2,3},{3,4},{4,5},{5,6},{6,7},{7,8},{8,9},{9,10},{10,1... | collective-permute-start | bytes 24584 | tf_op jit(solution)/shard_map/ppermute | solution.py:326

commit v4 on v3

--- a/solution.py
+++ b/solution.py
@@ -17,6 +17,7 @@
 LANES = 128
 ROWS = 8
 PIECES = 4
+ORDER = (8, 12, 3, 4, 6, 15, 10, 14, 13, 1, 9, 2, 5, 7, 0, 11)
 
 
 def pitch_coefficients(count, omega):
@@ -90,10 +91,10 @@
 
     for p in range(PIECES):
         for t in range(p * span, (p + 1) * span, ROWS):
-            values = [gathered_ref[i, t : t + ROWS, :] for i in range(INST)]
+            values = [gathered_ref[ORDER.index(i), t : t + ROWS, :] for i in range(INST)]
             outs = coupled(values[:ROTOR_INST], OMEGA_ROTOR) + coupled(values[ROTOR_INST:], OMEGA_STATOR)
             for i in range(INST):
-                held_ref[i, t : t + ROWS, :] = outs[i]
+                held_ref[ORDER.index(i), t : t + ROWS, :] = outs[i]
         if p < PIECES - 1:
             leave(p, p * span, span)
     for i, (want, first) in enumerate(zip(wants, firsts)):
@@ -224,7 +225,7 @@
     total = jnp.zeros((ROWS, LANES), jnp.float32)
     for i in range(INST):
         coef = jnp.where(inst0 == i, weight0, 0.0) + jnp.where(inst2 == i, weight2, 0.0)
-        total = total + coef * packed_ref[i, depth : depth + ROWS, :]
+        total = total + coef * packed_ref[ORDER.index(i), depth : depth + ROWS, :]
     ghost = total + pltpu.roll(total, 4, 0)
     ghost = [jnp.broadcast_to(ghost[c : c + 1, :], (ROWS, LANES)) for c in range(4)]
     flux_x, _ = fluxes(*ghost)
@@ -305,7 +306,7 @@
         cost_estimate=pl.CostEstimate(flops=0, bytes_accessed=32 << 20, transcendentals=0),
         name="edges",
     )(cells)
-    gathered = lax.all_to_all(sent, "inst", 0, 0)
+    gathered = lax.all_to_all(sent, "inst", 0, 0, axis_index_groups=[ORDER])
     faces = collected(export, "cell")
     packed = pl.pallas_call(
         source_kernel,
@@ -320,7 +321,7 @@
         name="source",
     )(gathered, faces)
     head, tail, packed = lax.optimization_barrier((head, tail, packed))
-    packed = lax.all_to_all(packed, "inst", 0, 0)
+    packed = lax.all_to_all(packed, "inst", 0, 0, axis_index_groups=[ORDER])
 
     right = lax.ppermute(head, "cell", [((i + 1) % cell_count, i) for i in range(cell_count)])
     left = lax.ppermute(tail, "cell", [(i, (i + 1) % cell_count) for i in range(cell_count)])

time: 57.9 us -> 56.2 us (0.971)
  the two profiles are of different devices: /device:TPU:64 before, /device:TPU:24 now
where the time goes in v4:
time: 56.2 us; the launch traced here: 56 us
  starting transfers between devices  29.1 us (52%)
  waiting for transfers between devices  16.7 us (30%)
  Pallas kernels  9.43 us (17%)
  between operations  0.72 us (1%)
    ppermute x6, starting transfers between devices, collected(): blocks.append(lax.ppermute(block, axis, pairs))  15.4 us
    all_to_all x1, starting transfers between devices, on_device(): packed = lax.all_to_all(packed, 'inst', 0, 0, axis_index_groups=[ORDER])  7.24 us
    all_to_all x1, waiting for transfers between devices, on_device(): packed = lax.all_to_all(packed, 'inst', 0, 0, axis_index_groups=[ORDER])  6.83 us
    all_to_all x1, starting transfers between devices, on_device(): gathered = lax.all_to_all(sent, 'inst', 0, 0, axis_index_groups=[ORDER])  5.92 us
    ppermute x6, waiting for transfers between devices, collected(): blocks.append(lax.ppermute(block, axis, pairs))  5.58 us
    pallas_call x1, Pallas kernels, on_device(): pl.pallas_call(partial_kernel, grid=(blocks,), out_shape=pltpu.VMEM(cells...  4.03 us
    ppermute x1, waiting for transfers between devices, on_device(): lax.ppermute(tail, 'cell', [(i, (i + 1) % cell_count) for i in range(cell...  2.92 us
    pallas_call x1, Pallas kernels, on_device(): pl.pallas_call(send_kernel, out_shape=jax.ShapeDtypeStruct((inst_count, d...  2.05 us
  transfers between devices with their start and end apart: 10, of which 5 were waited for; matrix products, arithmetic and copies ran while one was open for 0% of the time, Pallas kernels for 8%

profile of v4, /device:TPU:24, one launch (start us, length us, event | category | flops | bytes accessed | tf_op | source)
XLA Modules:
  0.0 56.0 jit_solution(1328917797493236407)
XLA Ops:
  0.6 2.1 %send.1 = f32[16,136,128]{2,1,0:T(8,128)} custom-call(f32[16,128,128]{2,1,0:T(8,128)} %bitcast.6, s32[4,1,128]{2,1,0:T(1,128)} %face_ref.1), custom_call_target="tpu_custom_call" | custom-call | tf_op jit(solution)/shard_map/send/pallas_call | solution.py:282
  2.7 0.0 copy-start
  2.7 5.9 %all-to-all-start = ((f32[16,136,128]{2,1,0:T(8,128)}), f32[16,136,128]{2,1,0:T(8,128)S(1)}, u32[]{:S(2)}, u32[]{:S(2)}) async-start(f32[16,136,128]{2,1,0:T(8,128)} %send.1), calls=%async_computation | async-start | bytes 2228224 | tf_op jit(solution)/shard_map/all_to_all | solution.py:309
  8.6 0.0 copy-done
  8.6 0.7 %edges.1 = (f32[8,128]{1,0:T(8,128)S(1)}, f32[4,512]{1,0:T(4,128)S(1)}, f32[4,512]{1,0:T(4,128)S(1)}) custom-call(f32[4,512,128]{2,1,0:T(8,128)S(1)} %bitcast.7), custom_call_target="tpu_custom_call" | custom-call | bytes 33554432 | tf_op jit(solution)/shard_map/edges/pallas_call | solution.py:296
  9.3 3.3 %collective-permute-start.2 = (f32[8,128]{1,0:T(8,128)S(1)}, f32[8,128]{1,0:T(8,128)S(1)}, u32[]{:S(2)}, u32[]{:S(2)}) collective-permute-start(f32[8,128]{1,0:T(8,128)S(1)} %get-tuple-element.16), channel_id=1, source_target_pairs={{12,0},{13,1},{14,2},{15,3},{0,4},{1,5},{2,6},{3,7},{4,8},{5,9},{6... | collective-permute-start | bytes 12296 | tf_op jit(solution)/shard_map/ppermute | solution.py:268
  12.7 5.4 %collective-permute-start.1 = (f32[8,128]{1,0:T(8,128)S(1)}, f32[8,128]{1,0:T(8,128)S(1)}, u32[]{:S(2)}, u32[]{:S(2)}) collective-permute-start(f32[8,128]{1,0:T(8,128)S(1)} %get-tuple-element.16), channel_id=1, source_target_pairs={{8,0},{9,1},{10,2},{11,3},{12,4},{13,5},{14,6},{15,7},{0,8},{1,9},... | collective-permute-start | bytes 12296 | tf_op jit(solution)/shard_map/ppermute | solution.py:268
  18.1 2.7 %collective-permute-start = (f32[8,128]{1,0:T(8,128)S(1)}, f32[8,128]{1,0:T(8,128)S(1)}, u32[]{:S(2)}, u32[]{:S(2)}) collective-permute-start(f32[8,128]{1,0:T(8,128)S(1)} %get-tuple-element.16), channel_id=1, source_target_pairs={{4,0},{5,1},{6,2},{7,3},{8,4},{9,5},{10,6},{11,7},{12,8},{13,9},{1... | collective-permute-start | bytes 12296 | tf_op jit(solution)/shard_map/ppermute | solution.py:268
  20.7 1.8 %collective-permute-done = f32[8,128]{1,0:T(8,128)S(1)} collective-permute-done((f32[8,128]{1,0:T(8,128)S(1)}, f32[8,128]{1,0:T(8,128)S(1)}, u32[]{:S(2)}, u32[]{:S(2)}) %collective-permute-start) | collective-permute-done | bytes 4128 | tf_op jit(solution)/shard_map/ppermute | solution.py:268
  22.6 0.0 collective-permute-done.1
  22.6 0.0 collective-permute-done.2
  22.6 0.9 %collective-permute-start.3 = (f32[32,128]{1,0:T(8,128)S(1)}, f32[32,128]{1,0:T(8,128)S(1)}, u32[]{:S(2)}, u32[]{:S(2)}) collective-permute-start(f32[32,128]{1,0:T(8,128)S(1)} %get-tuple-element.22), channel_id=1, source_target_pairs={{1,0},{2,1},{3,2},{4,3},{5,4},{6,5},{7,6},{8,7},{9,8},{10,9},{11,1... | collective-permute-start | bytes 49160 | tf_op jit(solution)/shard_map/ppermute | solution.py:268
  23.5 3.1 %collective-permute-start.5 = (f32[32,128]{1,0:T(8,128)S(1)}, f32[32,128]{1,0:T(8,128)S(1)}, u32[]{:S(2)}, u32[]{:S(2)}) collective-permute-start(f32[32,128]{1,0:T(8,128)S(1)} %get-tuple-element.22), channel_id=1, source_target_pairs={{3,0},{4,1},{5,2},{6,3},{7,4},{8,5},{9,6},{10,7},{11,8},{12,9},{13... | collective-permute-start | bytes 49160 | tf_op jit(solution)/shard_map/ppermute | solution.py:268
  26.6 0.0 collective-permute-start.4
  26.6 0.0 collective-permute-done.3
  26.6 3.7 %collective-permute-done.4 = f32[32,128]{1,0:T(8,128)S(1)} collective-permute-done((f32[32,128]{1,0:T(8,128)S(1)}, f32[32,128]{1,0:T(8,128)S(1)}, u32[]{:S(2)}, u32[]{:S(2)}) %collective-permute-start.4) | collective-permute-done | bytes 16416 | tf_op jit(solution)/shard_map/ppermute | solution.py:268
  30.3 0.0 collective-permute-done.5
  30.3 0.0 all-to-all-done.gathered_ref
  30.4 1.2 %source.1 = f32[16,136,128]{2,1,0:T(8,128)} custom-call(f32[16,136,128]{2,1,0:T(8,128)S(1)} %all-to-all-done.gathered_ref, f32[128,128]{1,0:T(8,128)S(1)} %constant_dynamic-update-slice_fusion.4.faces_ref), custom_call_target="tpu_custom_call" | custom-call | tf_op jit(solution)/shard_map/source/pallas_call | solution.py:311
  31.6 7.2 %all-to-all-start.1 = ((f32[16,136,128]{2,1,0:T(8,128)}), f32[16,136,128]{2,1,0:T(8,128)S(1)}, u32[]{:S(2)}, u32[]{:S(2)}) async-start(f32[16,136,128]{2,1,0:T(8,128)} %source.1), calls=%async_computation.1 | async-start | bytes 2228224 | tf_op jit(solution)/shard_map/all_to_all | solution.py:324
  38.8 0.0 copy-start.1
  38.8 0.0 copy-start.2
  38.8 0.5 collective-permute-start.6
  39.4 0.0 collective-permute-start.7
  39.4 1.4 %collective-permute-done.6.right_ref = f32[4,512]{1,0:T(4,128)S(1)} collective-permute-done((f32[4,512]{1,0:T(4,128)S(1)}, f32[4,512]{1,0:T(4,128)S(1)}, u32[]{:S(2)}, u32[]{:S(2)}) %collective-permute-start.6) | collective-permute-done | bytes 8224 | tf_op jit(solution)/shard_map/ppermute | solution.py:326
  40.7 2.9 %collective-permute-done.7.left_ref = f32[4,512]{1,0:T(4,128)S(1)} collective-permute-done((f32[4,512]{1,0:T(4,128)S(1)}, f32[4,512]{1,0:T(4,128)S(1)}, u32[]{:S(2)}, u32[]{:S(2)}) %collective-permute-start.7) | collective-permute-done | bytes 8224 | tf_op jit(solution)/shard_map/ppermute | solution.py:327
  43.6 4.0 %partial.1.partial_ref = f32[4,512,128]{2,1,0:T(8,128)S(1)} custom-call(f32[4,512,128]{2,1,0:T(8,128)S(1)} %bitcast.8, f32[4,512,128]{2,1,0:T(8,128)S(1)} %bitcast.9, f32[4,512,128]{2,1,0:T(8,128)S(1)} %bitcast.10, f32[4,512]{1,0:T(4,128)S(1)} %collective-permute-done.6.right_ref, f32[4,512]{1,0:T(4,128)S(1)} %collective-permute-done.7.left_ref), custom_call_target="tpu_custom_call" | custom-call | flops 26214400 | bytes 4194304 | tf_op jit(solution)/shard_map/partial/pallas_call | solution.py:334
  47.7 6.8 %all-to-all-done.1.packed_ref = f32[16,136,128]{2,1,0:T(8,128)S(1)} async-done(((f32[16,136,128]{2,1,0:T(8,128)}), f32[16,136,128]{2,1,0:T(8,128)S(1)}, u32[]{:S(2)}, u32[]{:S(2)}) %all-to-all-start.1) | async-done | bytes 1114144 | tf_op jit(solution)/shard_map/all_to_all | solution.py:324
  54.5 0.0 copy-done.1
  54.5 0.0 copy-done.2
  54.5 1.4 %finish.1 = (f32[4,512,128]{2,1,0:T(8,128)}, f32[4,512,128]{2,1,0:T(8,128)}) custom-call(f32[16,136,128]{2,1,0:T(8,128)S(1)} %all-to-all-done.1.packed_ref, f32[4,512,128]{2,1,0:T(8,128)S(1)} %partial.1.partial_ref, f32[4,512,128]{2,1,0:T(8,128)S(1)} %bitcast.11, s32[4,128]{1,0:T(4,128)S(1)} %bitcast.12, f32[4,128]{1,0:T(4,128)S(1)} %bitcast.13), custom_call_target="tpu_custom_call" | custom-call | tf_op jit(solution)/shard_map/finish/pallas_call | solution.py:355
  (7 shorter events, 0.0 us)
Async XLA Ops:
  2.7 5.9 %copy-start = (f32[1,4,512,128]{3,2,1,0:T(8,128)S(1)}, f32[1,4,512,128]{3,2,1,0:T(8,128)}, u32[]{:S(2)}) copy-start(f32[1,4,512,128]{3,2,1,0:T(8,128)} %param.4) | copy-start | bytes 3145732
  2.7 27.6 %all-to-all-start = ((f32[16,136,128]{2,1,0:T(8,128)}), f32[16,136,128]{2,1,0:T(8,128)S(1)}, u32[]{:S(2)}, u32[]{:S(2)}) async-start(f32[16,136,128]{2,1,0:T(8,128)} %send.1), calls=%async_computation | async-start | bytes 2228224 | tf_op jit(solution)/shard_map/all_to_all | solution.py:309
  9.3 13.3 %collective-permute-start.2 = (f32[8,128]{1,0:T(8,128)S(1)}, f32[8,128]{1,0:T(8,128)S(1)}, u32[]{:S(2)}, u32[]{:S(2)}) collective-permute-start(f32[8,128]{1,0:T(8,128)S(1)} %get-tuple-element.16), channel_id=1, source_target_pairs={{12,0},{13,1},{14,2},{15,3},{0,4},{1,5},{2,6},{3,7},{4,8},{5,9},{6... | collective-permute-start | bytes 12296 | tf_op jit(solution)/shard_map/ppermute | solution.py:268
  12.7 9.9 %collective-permute-start.1 = (f32[8,128]{1,0:T(8,128)S(1)}, f32[8,128]{1,0:T(8,128)S(1)}, u32[]{:S(2)}, u32[]{:S(2)}) collective-permute-start(f32[8,128]{1,0:T(8,128)S(1)} %get-tuple-element.16), channel_id=1, source_target_pairs={{8,0},{9,1},{10,2},{11,3},{12,4},{13,5},{14,6},{15,7},{0,8},{1,9},... | collective-permute-start | bytes 12296 | tf_op jit(solution)/shard_map/ppermute | solution.py:268
  18.1 4.5 %collective-permute-start = (f32[8,128]{1,0:T(8,128)S(1)}, f32[8,128]{1,0:T(8,128)S(1)}, u32[]{:S(2)}, u32[]{:S(2)}) collective-permute-start(f32[8,128]{1,0:T(8,128)S(1)} %get-tuple-element.16), channel_id=1, source_target_pairs={{4,0},{5,1},{6,2},{7,3},{8,4},{9,5},{10,6},{11,7},{12,8},{13,9},{1... | collective-permute-start | bytes 12296 | tf_op jit(solution)/shard_map/ppermute | solution.py:268
  22.6 4.0 %collective-permute-start.3 = (f32[32,128]{1,0:T(8,128)S(1)}, f32[32,128]{1,0:T(8,128)S(1)}, u32[]{:S(2)}, u32[]{:S(2)}) collective-permute-start(f32[32,128]{1,0:T(8,128)S(1)} %get-tuple-element.22), channel_id=1, source_target_pairs={{1,0},{2,1},{3,2},{4,3},{5,4},{6,5},{7,6},{8,7},{9,8},{10,9},{11,1... | collective-permute-start | bytes 49160 | tf_op jit(solution)/shard_map/ppermute | solution.py:268
  23.5 6.8 %collective-permute-start.5 = (f32[32,128]{1,0:T(8,128)S(1)}, f32[32,128]{1,0:T(8,128)S(1)}, u32[]{:S(2)}, u32[]{:S(2)}) collective-permute-start(f32[32,128]{1,0:T(8,128)S(1)} %get-tuple-element.22), channel_id=1, source_target_pairs={{3,0},{4,1},{5,2},{6,3},{7,4},{8,5},{9,6},{10,7},{11,8},{12,9},{13... | collective-permute-start | bytes 49160 | tf_op jit(solution)/shard_map/ppermute | solution.py:268
  26.6 3.7 %collective-permute-start.4 = (f32[32,128]{1,0:T(8,128)S(1)}, f32[32,128]{1,0:T(8,128)S(1)}, u32[]{:S(2)}, u32[]{:S(2)}) collective-permute-start(f32[32,128]{1,0:T(8,128)S(1)} %get-tuple-element.22), channel_id=1, source_target_pairs={{2,0},{3,1},{4,2},{5,3},{6,4},{7,5},{8,6},{9,7},{10,8},{11,9},{12,... | collective-permute-start | bytes 49160 | tf_op jit(solution)/shard_map/ppermute | solution.py:268
  31.6 22.9 %all-to-all-start.1 = ((f32[16,136,128]{2,1,0:T(8,128)}), f32[16,136,128]{2,1,0:T(8,128)S(1)}, u32[]{:S(2)}, u32[]{:S(2)}) async-start(f32[16,136,128]{2,1,0:T(8,128)} %source.1), calls=%async_computation.1 | async-start | bytes 2228224 | tf_op jit(solution)/shard_map/all_to_all | solution.py:324
  38.8 15.7 %copy-start.1 = (s32[4,1,128]{2,1,0:T(1,128)S(1)}, s32[4,1,128]{2,1,0:T(1,128)}, u32[]{:S(2)}) copy-start(s32[4,1,128]{2,1,0:T(1,128)} %param.5) | copy-start | bytes 6148
  38.8 15.7 %copy-start.2 = (f32[4,1,128]{2,1,0:T(1,128)S(1)}, f32[4,1,128]{2,1,0:T(1,128)}, u32[]{:S(2)}) copy-start(f32[4,1,128]{2,1,0:T(1,128)} %param.7) | copy-start | bytes 6148
  38.8 1.9 %collective-permute-start.6 = (f32[4,512]{1,0:T(4,128)S(1)}, f32[4,512]{1,0:T(4,128)S(1)}, u32[]{:S(2)}, u32[]{:S(2)}) collective-permute-start(f32[4,512]{1,0:T(4,128)S(1)} %get-tuple-element.18), channel_id=1, source_target_pairs={{1,0},{2,1},{3,2},{4,3},{5,4},{6,5},{7,6},{8,7},{9,8},{10,9},{11,1... | collective-permute-start | bytes 24584 | tf_op jit(solution)/shard_map/ppermute | solution.py:326
  39.4 4.3 %collective-permute-start.7 = (f32[4,512]{1,0:T(4,128)S(1)}, f32[4,512]{1,0:T(4,128)S(1)}, u32[]{:S(2)}, u32[]{:S(2)}) collective-permute-start(f32[4,512]{1,0:T(4,128)S(1)} %get-tuple-element.19), channel_id=1, source_target_pairs={{0,1},{1,2},{2,3},{3,4},{4,5},{5,6},{6,7},{7,8},{8,9},{9,10},{10,1... | collective-permute-start | bytes 24584 | tf_op jit(solution)/shard_map/ppermute | solution.py:327

commit v5 on v4

--- a/solution.py
+++ b/solution.py
@@ -83,7 +83,7 @@
         leaving.append(copy)
 
     def tile(ahead):
-        place = (ahead & 3) * (slabs // 4) + (ahead >> 2)
+        place = ahead
         return faces_ref[pl.ds(pl.multiple_of(place * ROWS, ROWS), ROWS), :]
 
     wants = [gathered_ref[i, depth : depth + ROWS, :].astype(jnp.int32) for i in range(INST)]
@@ -261,7 +261,7 @@
 
 def collected(block, axis):
     count = lax.axis_size(axis)
-    for step in (count // 4, 1):
+    for step in (1, count // 4):
         blocks = [block]
         for k in range(1, 4):
             pairs = [((i + k * step) % count, i) for i in range(count)]
@@ -307,7 +307,8 @@
         name="edges",
     )(cells)
     gathered = lax.all_to_all(sent, "inst", 0, 0, axis_index_groups=[ORDER])
-    faces = collected(export, "cell")
+    faces = collected(export[:4], "cell").reshape(cell_count, 4, width)
+    faces = jnp.concatenate([faces, faces], 1).reshape(cell_count * ROWS, width)
     packed = pl.pallas_call(
         source_kernel,
         out_shape=jax.ShapeDtypeStruct((inst_count, depth + ROWS, width), jnp.float32),

time: 56.2 us -> 54.3 us (0.966)
  the two profiles are of different devices: /device:TPU:24 before, /device:TPU:64 now
where the time goes in v5:
time: 54.3 us; the launch traced here: 53.8 us
  starting transfers between devices  27.2 us (50%)
  waiting for transfers between devices  16.4 us (30%)
  Pallas kernels  9.44 us (17%)
  between operations  0.72 us (1%)
    ppermute x6, starting transfers between devices, collected(): blocks.append(lax.ppermute(block, axis, pairs))  11.1 us
    all_to_all x1, starting transfers between devices, on_device(): gathered = lax.all_to_all(sent, 'inst', 0, 0, axis_index_groups=[ORDER])  8.38 us
    all_to_all x1, starting transfers between devices, on_device(): packed = lax.all_to_all(packed, 'inst', 0, 0, axis_index_groups=[ORDER])  7.24 us
    all_to_all x1, waiting for transfers between devices, on_device(): packed = lax.all_to_all(packed, 'inst', 0, 0, axis_index_groups=[ORDER])  6.97 us
    ppermute x6, waiting for transfers between devices, collected(): blocks.append(lax.ppermute(block, axis, pairs))  6.83 us
    pallas_call x1, Pallas kernels, on_device(): pl.pallas_call(partial_kernel, grid=(blocks,), out_shape=pltpu.VMEM(cells...  4.03 us
    pallas_call x1, Pallas kernels, on_device(): pl.pallas_call(send_kernel, out_shape=jax.ShapeDtypeStruct((inst_count, d...  2.06 us
    ppermute x1, waiting for transfers between devices, on_device(): lax.ppermute(tail, 'cell', [(i, (i + 1) % cell_count) for i in range(cell...  1.73 us
  transfers between devices with their start and end apart: 10, of which 7 were waited for; matrix products, arithmetic and copies ran while one was open for 0% of the time, Pallas kernels for 9%

profile of v5, /device:TPU:64, one launch (start us, length us, event | category | flops | bytes accessed | tf_op | source)
XLA Modules:
  0.0 53.8 jit_solution(2821575365687480350)
XLA Ops:
  0.6 2.1 %send.1 = f32[16,136,128]{2,1,0:T(8,128)} custom-call(f32[16,128,128]{2,1,0:T(8,128)} %bitcast.9, s32[4,1,128]{2,1,0:T(1,128)} %face_ref.1), custom_call_target="tpu_custom_call" | custom-call | tf_op jit(solution)/shard_map/send/pallas_call | solution.py:282
  2.7 0.0 copy-start
  2.7 8.4 %all-to-all-start = ((f32[16,136,128]{2,1,0:T(8,128)}), f32[16,136,128]{2,1,0:T(8,128)S(1)}, u32[]{:S(2)}, u32[]{:S(2)}) async-start(f32[16,136,128]{2,1,0:T(8,128)} %send.1), calls=%async_computation | async-start | bytes 2228224 | tf_op jit(solution)/shard_map/all_to_all | solution.py:309
  11.1 0.0 copy-done
  11.1 0.7 %edges.1 = (f32[8,128]{1,0:T(8,128)S(1)}, f32[4,512]{1,0:T(4,128)S(1)}, f32[4,512]{1,0:T(4,128)S(1)}) custom-call(f32[4,512,128]{2,1,0:T(8,128)S(1)} %bitcast.10), custom_call_target="tpu_custom_call" | custom-call | bytes 33554432 | tf_op jit(solution)/shard_map/edges/pallas_call | solution.py:296
  11.8 0.1 collective-permute-start.2
  11.9 4.4 %collective-permute-start.1 = (f32[4,128]{1,0:T(4,128)S(1)}, f32[4,128]{1,0:T(4,128)S(1)}, u32[]{:S(2)}, u32[]{:S(2)}) collective-permute-start(f32[4,128]{1,0:T(4,128)S(1)} %slice.3), channel_id=1, source_target_pairs={{2,0},{3,1},{4,2},{5,3},{6,4},{7,5},{8,6},{9,7},{10,8},{11,9},{12,... | collective-permute-start | bytes 6152 | tf_op jit(solution)/shard_map/ppermute | solution.py:268
  16.3 1.1 %collective-permute-start = (f32[4,128]{1,0:T(4,128)S(1)}, f32[4,128]{1,0:T(4,128)S(1)}, u32[]{:S(2)}, u32[]{:S(2)}) collective-permute-start(f32[4,128]{1,0:T(4,128)S(1)} %slice.3), channel_id=1, source_target_pairs={{1,0},{2,1},{3,2},{4,3},{5,4},{6,5},{7,6},{8,7},{9,8},{10,9},{11,1... | collective-permute-start | bytes 6152 | tf_op jit(solution)/shard_map/ppermute | solution.py:268
  17.4 0.0 collective-permute-done.2
  17.4 0.2 collective-permute-done.1
  17.6 1.1 %collective-permute-done = f32[4,128]{1,0:T(4,128)S(1)} collective-permute-done((f32[4,128]{1,0:T(4,128)S(1)}, f32[4,128]{1,0:T(4,128)S(1)}, u32[]{:S(2)}, u32[]{:S(2)}) %collective-permute-start) | collective-permute-done | bytes 2080 | tf_op jit(solution)/shard_map/ppermute | solution.py:268
  18.7 1.4 %collective-permute-start.5 = (f32[16,128]{1,0:T(8,128)S(1)}, f32[16,128]{1,0:T(8,128)S(1)}, u32[]{:S(2)}, u32[]{:S(2)}) collective-permute-start(f32[16,128]{1,0:T(8,128)S(1)} %pad_maximum_fusion), channel_id=1, source_target_pairs={{12,0},{13,1},{14,2},{15,3},{0,4},{1,5},{2,6},{3,7},{4,8},{5,9},{6... | collective-permute-start | bytes 24584 | tf_op jit(solution)/shard_map/ppermute | solution.py:268
  20.1 3.8 %collective-permute-start.4 = (f32[16,128]{1,0:T(8,128)S(1)}, f32[16,128]{1,0:T(8,128)S(1)}, u32[]{:S(2)}, u32[]{:S(2)}) collective-permute-start(f32[16,128]{1,0:T(8,128)S(1)} %pad_maximum_fusion), channel_id=1, source_target_pairs={{8,0},{9,1},{10,2},{11,3},{12,4},{13,5},{14,6},{15,7},{0,8},{1,9},... | collective-permute-start | bytes 24584 | tf_op jit(solution)/shard_map/ppermute | solution.py:268
  24.0 0.2 collective-permute-start.3
  24.2 0.0 collective-permute-done.5
  24.2 3.5 %collective-permute-done.4 = f32[16,128]{1,0:T(8,128)S(1)} collective-permute-done((f32[16,128]{1,0:T(8,128)S(1)}, f32[16,128]{1,0:T(8,128)S(1)}, u32[]{:S(2)}, u32[]{:S(2)}) %collective-permute-start.4) | collective-permute-done | bytes 8224 | tf_op jit(solution)/shard_map/ppermute | solution.py:268
  27.7 2.0 %collective-permute-done.3 = f32[16,128]{1,0:T(8,128)S(1)} collective-permute-done((f32[16,128]{1,0:T(8,128)S(1)}, f32[16,128]{1,0:T(8,128)S(1)}, u32[]{:S(2)}, u32[]{:S(2)}) %collective-permute-start.3) | collective-permute-done | bytes 8224 | tf_op jit(solution)/shard_map/ppermute | solution.py:268
  29.8 0.0 all-to-all-done.gathered_ref
  29.8 1.2 %source.1 = f32[16,136,128]{2,1,0:T(8,128)} custom-call(f32[16,136,128]{2,1,0:T(8,128)S(1)} %all-to-all-done.gathered_ref, f32[128,128]{1,0:T(8,128)S(1)} %maximum_bitcast_fusion.faces_ref), custom_call_target="tpu_custom_call" | custom-call | tf_op jit(solution)/shard_map/source/pallas_call | solution.py:312
  31.0 7.2 %all-to-all-start.1 = ((f32[16,136,128]{2,1,0:T(8,128)}), f32[16,136,128]{2,1,0:T(8,128)S(1)}, u32[]{:S(2)}, u32[]{:S(2)}) async-start(f32[16,136,128]{2,1,0:T(8,128)} %source.1), calls=%async_computation.1 | async-start | bytes 2228224 | tf_op jit(solution)/shard_map/all_to_all | solution.py:325
  38.2 0.0 copy-start.1
  38.2 0.0 copy-start.2
  38.3 0.0 collective-permute-start.6
  38.3 0.5 collective-permute-start.7
  38.8 0.9 %collective-permute-done.6.right_ref = f32[4,512]{1,0:T(4,128)S(1)} collective-permute-done((f32[4,512]{1,0:T(4,128)S(1)}, f32[4,512]{1,0:T(4,128)S(1)}, u32[]{:S(2)}, u32[]{:S(2)}) %collective-permute-start.6) | collective-permute-done | bytes 8224 | tf_op jit(solution)/shard_map/ppermute | solution.py:327
  39.6 1.7 %collective-permute-done.7.left_ref = f32[4,512]{1,0:T(4,128)S(1)} collective-permute-done((f32[4,512]{1,0:T(4,128)S(1)}, f32[4,512]{1,0:T(4,128)S(1)}, u32[]{:S(2)}, u32[]{:S(2)}) %collective-permute-start.7) | collective-permute-done | bytes 8224 | tf_op jit(solution)/shard_map/ppermute | solution.py:328
  41.4 4.0 %partial.1.partial_ref = f32[4,512,128]{2,1,0:T(8,128)S(1)} custom-call(f32[4,512,128]{2,1,0:T(8,128)S(1)} %bitcast.11, f32[4,512,128]{2,1,0:T(8,128)S(1)} %bitcast.12, f32[4,512,128]{2,1,0:T(8,128)S(1)} %bitcast.13, f32[4,512]{1,0:T(4,128)S(1)} %collective-permute-done.6.right_ref, f32[4,512]{1,0:T(4,128)S(1)} %collective-permute-done.7.left_ref), custom_call_target="tpu_custom_call" | custom-call | flops 26214400 | bytes 4194304 | tf_op jit(solution)/shard_map/partial/pallas_call | solution.py:335
  45.4 7.0 %all-to-all-done.1.packed_ref = f32[16,136,128]{2,1,0:T(8,128)S(1)} async-done(((f32[16,136,128]{2,1,0:T(8,128)}), f32[16,136,128]{2,1,0:T(8,128)S(1)}, u32[]{:S(2)}, u32[]{:S(2)}) %all-to-all-start.1) | async-done | bytes 1114144 | tf_op jit(solution)/shard_map/all_to_all | solution.py:325
  52.4 0.0 copy-done.1
  52.4 0.0 copy-done.2
  52.4 1.5 %finish.1 = (f32[4,512,128]{2,1,0:T(8,128)}, f32[4,512,128]{2,1,0:T(8,128)}) custom-call(f32[16,136,128]{2,1,0:T(8,128)S(1)} %all-to-all-done.1.packed_ref, f32[4,512,128]{2,1,0:T(8,128)S(1)} %partial.1.partial_ref, f32[4,512,128]{2,1,0:T(8,128)S(1)} %bitcast.14, s32[4,128]{1,0:T(4,128)S(1)} %bitcast.15, f32[4,128]{1,0:T(4,128)S(1)} %bitcast.16), custom_call_target="tpu_custom_call" | custom-call | tf_op jit(solution)/shard_map/finish/pallas_call | solution.py:356
  (4 shorter events, 0.1 us)
Async XLA Ops:
  2.7 8.4 %copy-start = (f32[1,4,512,128]{3,2,1,0:T(8,128)S(1)}, f32[1,4,512,128]{3,2,1,0:T(8,128)}, u32[]{:S(2)}) copy-start(f32[1,4,512,128]{3,2,1,0:T(8,128)} %param.4) | copy-start | bytes 3145732
  2.7 27.1 %all-to-all-start = ((f32[16,136,128]{2,1,0:T(8,128)}), f32[16,136,128]{2,1,0:T(8,128)S(1)}, u32[]{:S(2)}, u32[]{:S(2)}) async-start(f32[16,136,128]{2,1,0:T(8,128)} %send.1), calls=%async_computation | async-start | bytes 2228224 | tf_op jit(solution)/shard_map/all_to_all | solution.py:309
  11.8 5.6 %collective-permute-start.2 = (f32[4,128]{1,0:T(4,128)S(1)}, f32[4,128]{1,0:T(4,128)S(1)}, u32[]{:S(2)}, u32[]{:S(2)}) collective-permute-start(f32[4,128]{1,0:T(4,128)S(1)} %slice.3), channel_id=1, source_target_pairs={{3,0},{4,1},{5,2},{6,3},{7,4},{8,5},{9,6},{10,7},{11,8},{12,9},{13... | collective-permute-start | bytes 6152 | tf_op jit(solution)/shard_map/ppermute | solution.py:268
  11.9 5.7 %collective-permute-start.1 = (f32[4,128]{1,0:T(4,128)S(1)}, f32[4,128]{1,0:T(4,128)S(1)}, u32[]{:S(2)}, u32[]{:S(2)}) collective-permute-start(f32[4,128]{1,0:T(4,128)S(1)} %slice.3), channel_id=1, source_target_pairs={{2,0},{3,1},{4,2},{5,3},{6,4},{7,5},{8,6},{9,7},{10,8},{11,9},{12,... | collective-permute-start | bytes 6152 | tf_op jit(solution)/shard_map/ppermute | solution.py:268
  16.3 2.4 %collective-permute-start = (f32[4,128]{1,0:T(4,128)S(1)}, f32[4,128]{1,0:T(4,128)S(1)}, u32[]{:S(2)}, u32[]{:S(2)}) collective-permute-start(f32[4,128]{1,0:T(4,128)S(1)} %slice.3), channel_id=1, source_target_pairs={{1,0},{2,1},{3,2},{4,3},{5,4},{6,5},{7,6},{8,7},{9,8},{10,9},{11,1... | collective-permute-start | bytes 6152 | tf_op jit(solution)/shard_map/ppermute | solution.py:268
  18.7 5.5 %collective-permute-start.5 = (f32[16,128]{1,0:T(8,128)S(1)}, f32[16,128]{1,0:T(8,128)S(1)}, u32[]{:S(2)}, u32[]{:S(2)}) collective-permute-start(f32[16,128]{1,0:T(8,128)S(1)} %pad_maximum_fusion), channel_id=1, source_target_pairs={{12,0},{13,1},{14,2},{15,3},{0,4},{1,5},{2,6},{3,7},{4,8},{5,9},{6... | collective-permute-start | bytes 24584 | tf_op jit(solution)/shard_map/ppermute | solution.py:268
  20.1 7.6 %collective-permute-start.4 = (f32[16,128]{1,0:T(8,128)S(1)}, f32[16,128]{1,0:T(8,128)S(1)}, u32[]{:S(2)}, u32[]{:S(2)}) collective-permute-start(f32[16,128]{1,0:T(8,128)S(1)} %pad_maximum_fusion), channel_id=1, source_target_pairs={{8,0},{9,1},{10,2},{11,3},{12,4},{13,5},{14,6},{15,7},{0,8},{1,9},... | collective-permute-start | bytes 24584 | tf_op jit(solution)/shard_map/ppermute | solution.py:268
  24.0 5.8 %collective-permute-start.3 = (f32[16,128]{1,0:T(8,128)S(1)}, f32[16,128]{1,0:T(8,128)S(1)}, u32[]{:S(2)}, u32[]{:S(2)}) collective-permute-start(f32[16,128]{1,0:T(8,128)S(1)} %pad_maximum_fusion), channel_id=1, source_target_pairs={{4,0},{5,1},{6,2},{7,3},{8,4},{9,5},{10,6},{11,7},{12,8},{13,9},{1... | collective-permute-start | bytes 24584 | tf_op jit(solution)/shard_map/ppermute | solution.py:268
  31.0 21.4 %all-to-all-start.1 = ((f32[16,136,128]{2,1,0:T(8,128)}), f32[16,136,128]{2,1,0:T(8,128)S(1)}, u32[]{:S(2)}, u32[]{:S(2)}) async-start(f32[16,136,128]{2,1,0:T(8,128)} %source.1), calls=%async_computation.1 | async-start | bytes 2228224 | tf_op jit(solution)/shard_map/all_to_all | solution.py:325
  38.2 14.1 %copy-start.1 = (s32[4,1,128]{2,1,0:T(1,128)S(1)}, s32[4,1,128]{2,1,0:T(1,128)}, u32[]{:S(2)}) copy-start(s32[4,1,128]{2,1,0:T(1,128)} %param.5) | copy-start | bytes 6148
  38.2 14.1 %copy-start.2 = (f32[4,1,128]{2,1,0:T(1,128)S(1)}, f32[4,1,128]{2,1,0:T(1,128)}, u32[]{:S(2)}) copy-start(f32[4,1,128]{2,1,0:T(1,128)} %param.7) | copy-start | bytes 6148
  38.3 1.4 %collective-permute-start.6 = (f32[4,512]{1,0:T(4,128)S(1)}, f32[4,512]{1,0:T(4,128)S(1)}, u32[]{:S(2)}, u32[]{:S(2)}) collective-permute-start(f32[4,512]{1,0:T(4,128)S(1)} %get-tuple-element.18), channel_id=1, source_target_pairs={{1,0},{2,1},{3,2},{4,3},{5,4},{6,5},{7,6},{8,7},{9,8},{10,9},{11,1... | collective-permute-start | bytes 24584 | tf_op jit(solution)/shard_map/ppermute | solution.py:327
  38.3 3.1 %collective-permute-start.7 = (f32[4,512]{1,0:T(4,128)S(1)}, f32[4,512]{1,0:T(4,128)S(1)}, u32[]{:S(2)}, u32[]{:S(2)}) collective-permute-start(f32[4,512]{1,0:T(4,128)S(1)} %get-tuple-element.19), channel_id=1, source_target_pairs={{0,1},{1,2},{2,3},{3,4},{4,5},{5,6},{6,7},{7,8},{8,9},{9,10},{10,1... | collective-permute-start | bytes 24584 | tf_op jit(solution)/shard_map/ppermute | solution.py:328

commit v6 on v5

--- a/solution.py
+++ b/solution.py
@@ -17,7 +17,8 @@
 LANES = 128
 ROWS = 8
 PIECES = 4
-ORDER = (8, 12, 3, 4, 6, 15, 10, 14, 13, 1, 9, 2, 5, 7, 0, 11)
+SPREAD = (8, 12, 3, 4, 6, 15, 10, 14, 13, 1, 9, 2, 5, 7, 0, 11)
+COLLECT = (0, 4, 8, 12, 2, 6, 10, 14, 1, 5, 9, 13, 3, 7, 11, 15)
 
 
 def pitch_coefficients(count, omega):
@@ -91,10 +92,10 @@
 
     for p in range(PIECES):
         for t in range(p * span, (p + 1) * span, ROWS):
-            values = [gathered_ref[ORDER.index(i), t : t + ROWS, :] for i in range(INST)]
+            values = [gathered_ref[SPREAD.index(i), t : t + ROWS, :] for i in range(INST)]
             outs = coupled(values[:ROTOR_INST], OMEGA_ROTOR) + coupled(values[ROTOR_INST:], OMEGA_STATOR)
             for i in range(INST):
-                held_ref[ORDER.index(i), t : t + ROWS, :] = outs[i]
+                held_ref[COLLECT.index(i), t : t + ROWS, :] = outs[i]
         if p < PIECES - 1:
             leave(p, p * span, span)
     for i, (want, first) in enumerate(zip(wants, firsts)):
@@ -102,7 +103,7 @@
         place = want & (LANES - 1)
         here = jnp.take_along_axis(tile(ahead), place, axis=1, mode="promise_in_bounds")
         after = jnp.take_along_axis(tile((ahead + 1) & (slabs - 1)), place, axis=1, mode="promise_in_bounds")
-        held_ref[i, depth : depth + ROWS, :] = jnp.where((want >> 7) == first, here, after)
+        held_ref[COLLECT.index(SPREAD[i]), depth : depth + ROWS, :] = jnp.where((want >> 7) == first, here, after)
     leave(PIECES - 1, depth - span, span + ROWS)
     for copy in leaving:
         copy.wait()
@@ -120,13 +121,8 @@
     return (m, ma + p, mb, h * a), (n, mb, nb + p, h * b)
 
 
-def edge_kernel(cells_ref, export_ref, head_ref, tail_ref):
+def edge_kernel(cells_ref, head_ref, tail_ref):
     axial = cells_ref.shape[1]
-    rotor = lax.axis_index("inst") < ROTOR_INST
-    for c in range(4):
-        row = jnp.where(rotor, cells_ref[c, axial - 1 : axial, :], cells_ref[c, 0:1, :])
-        export_ref[c : c + 1, :] = row
-        export_ref[4 + c : 5 + c, :] = row
     lane = lax.broadcasted_iota(jnp.int32, (LANES, LANES), 1)
     for first in range(0, axial, LANES):
         span = pl.ds(first, LANES)
@@ -225,7 +221,7 @@
     total = jnp.zeros((ROWS, LANES), jnp.float32)
     for i in range(INST):
         coef = jnp.where(inst0 == i, weight0, 0.0) + jnp.where(inst2 == i, weight2, 0.0)
-        total = total + coef * packed_ref[ORDER.index(i), depth : depth + ROWS, :]
+        total = total + coef * packed_ref[COLLECT.index(i), depth : depth + ROWS, :]
     ghost = total + pltpu.roll(total, 4, 0)
     ghost = [jnp.broadcast_to(ghost[c : c + 1, :], (ROWS, LANES)) for c in range(4)]
     flux_x, _ = fluxes(*ghost)
@@ -241,7 +237,7 @@
             def strip(t, carry, c=c, j=j):
                 rows = pl.ds(pl.multiple_of(j * depth + t * ROWS, ROWS), ROWS)
                 mine = pl.ds(pl.multiple_of(t * ROWS, ROWS), ROWS)
-                out = partial_ref[c, rows, :] + packed_ref[c * per + j, mine, :]
+                out = partial_ref[c, rows, :] + packed_ref[COLLECT.index(SPREAD[c * per + j]), mine, :]
                 res_ref[c, rows, :] = out
                 next_ref[c, rows, :] = cells_ref[c, rows, :] - PSEUDO_STEP * out
                 return carry
@@ -293,21 +289,22 @@
         name="send",
     )(cells.reshape(inst_count, depth, width), src_face)
     sent, cells = lax.optimization_barrier((sent, cells))
-    export, head, tail = pl.pallas_call(
+    rotor = lax.axis_index("inst") < ROTOR_INST
+    export = jnp.where(rotor, cells[:, -1, :], cells[:, 0, :])
+    head, tail = pl.pallas_call(
         edge_kernel,
         out_shape=[
-            jax.ShapeDtypeStruct((ROWS, width), jnp.float32),
             jax.ShapeDtypeStruct((4, axial), jnp.float32),
             jax.ShapeDtypeStruct((4, axial), jnp.float32),
         ],
         in_specs=[vmem],
-        out_specs=[vmem] * 3,
+        out_specs=[vmem] * 2,
         compiler_params=pltpu.CompilerParams(vmem_limit_bytes=16 << 20),
         cost_estimate=pl.CostEstimate(flops=0, bytes_accessed=32 << 20, transcendentals=0),
         name="edges",
     )(cells)
-    gathered = lax.all_to_all(sent, "inst", 0, 0, axis_index_groups=[ORDER])
-    faces = collected(export[:4], "cell").reshape(cell_count, 4, width)
+    gathered = lax.all_to_all(sent, "inst", 0, 0, axis_index_groups=[SPREAD])
+    faces = collected(export, "cell").reshape(cell_count, 4, width)
     faces = jnp.concatenate([faces, faces], 1).reshape(cell_count * ROWS, width)
     packed = pl.pallas_call(
         source_kernel,
@@ -322,7 +319,7 @@
         name="source",
     )(gathered, faces)
     head, tail, packed = lax.optimization_barrier((head, tail, packed))
-    packed = lax.all_to_all(packed, "inst", 0, 0, axis_index_groups=[ORDER])
+    packed = lax.all_to_all(packed, "inst", 0, 0, axis_index_groups=[COLLECT])
 
     right = lax.ppermute(head, "cell", [((i + 1) % cell_count, i) for i in range(cell_count)])
     left = lax.ppermute(tail, "cell", [(i, (i + 1) % cell_count) for i in range(cell_count)])

time: 54.3 us -> 53.5 us (0.985)
  starting transfers between devices: 27.2 us -> 24.3 us
  waiting for transfers between devices: 16.4 us -> 18.6 us
    all_to_all x2, waiting for transfers between devices: 6.97 us -> 9.88 us  [the longest x1 9.88 us: on_device(): packed = lax.all_to_all(packed, 'inst', 0, 0, axis_index_groups=[COLLECT])]
    all_to_all x2, starting transfers between devices: 15.6 us -> 12.7 us  [the longest x1 8.38 us: on_device(): gathered = lax.all_to_all(sent, 'inst', 0, 0, axis_index_groups=[SPREAD])]
    ppermute x6, waiting for transfers between devices: 6.83 us -> 6.13 us  [collected(): blocks.append(lax.ppermute(block, axis, pairs))]
where the time goes in v6:
time: 53.5 us; the launch traced here: 53.2 us
  starting transfers between devices  24.3 us (45%)
  waiting for transfers between devices  18.6 us (35%)
  Pallas kernels  9.43 us (18%)
  between operations  0.74 us (1%)
    ppermute x6, starting transfers between devices, collected(): blocks.append(lax.ppermute(block, axis, pairs))  11.1 us
    all_to_all x1, waiting for transfers between devices, on_device(): packed = lax.all_to_all(packed, 'inst', 0, 0, axis_index_groups=[COLLECT])  9.88 us
    all_to_all x1, starting transfers between devices, on_device(): gathered = lax.all_to_all(sent, 'inst', 0, 0, axis_index_groups=[SPREAD])  8.38 us
    ppermute x6, waiting for transfers between devices, collected(): blocks.append(lax.ppermute(block, axis, pairs))  6.13 us
    all_to_all x1, starting transfers between devices, on_device(): packed = lax.all_to_all(packed, 'inst', 0, 0, axis_index_groups=[COLLECT])  4.36 us
    pallas_call x1, Pallas kernels, on_device(): pl.pallas_call(partial_kernel, grid=(blocks,), out_shape=pltpu.VMEM(cells...  4.03 us
    pallas_call x1, Pallas kernels, on_device(): pl.pallas_call(send_kernel, out_shape=jax.ShapeDtypeStruct((inst_count, d...  2.06 us
    ppermute x1, waiting for transfers between devices, on_device(): lax.ppermute(tail, 'cell', [(i, (i + 1) % cell_count) for i in range(cell...  1.73 us
  transfers between devices with their start and end apart: 10, of which 7 were waited for; matrix products, arithmetic and copies ran while one was open for 0% of the time, Pallas kernels for 9%

profile of v6, /device:TPU:64, one launch (start us, length us, event | category | flops | bytes accessed | tf_op | source)
XLA Modules:
  0.0 53.2 jit_solution(12528403685001226807)
XLA Ops:
  0.6 2.1 %send.1 = f32[16,136,128]{2,1,0:T(8,128)} custom-call(f32[16,128,128]{2,1,0:T(8,128)} %bitcast.10, s32[4,1,128]{2,1,0:T(1,128)} %face_ref.1), custom_call_target="tpu_custom_call" | custom-call | tf_op jit(solution)/shard_map/send/pallas_call | solution.py:278
  2.7 0.0 copy-start
  2.7 8.4 %all-to-all-start = ((f32[16,136,128]{2,1,0:T(8,128)}), f32[16,136,128]{2,1,0:T(8,128)S(1)}, u32[]{:S(2)}, u32[]{:S(2)}) async-start(f32[16,136,128]{2,1,0:T(8,128)} %send.1), calls=%async_computation | async-start | bytes 2228224 | tf_op jit(solution)/shard_map/all_to_all | solution.py:306
  11.1 0.0 copy-done
  11.1 0.1 collective-permute-start.2
  11.2 4.4 %collective-permute-start.1 = (f32[4,128]{1,0:T(4,128)S(1)}, f32[4,128]{1,0:T(4,128)S(1)}, u32[]{:S(2)}, u32[]{:S(2)}) collective-permute-start(f32[4,128]{1,0:T(4,128)S(1)} %bitcast.21), channel_id=1, source_target_pairs={{2,0},{3,1},{4,2},{5,3},{6,4},{7,5},{8,6},{9,7},{10,8},{11,9},{12,... | collective-permute-start | bytes 6152 | tf_op jit(solution)/shard_map/ppermute | solution.py:264
  15.6 1.1 %collective-permute-start = (f32[4,128]{1,0:T(4,128)S(1)}, f32[4,128]{1,0:T(4,128)S(1)}, u32[]{:S(2)}, u32[]{:S(2)}) collective-permute-start(f32[4,128]{1,0:T(4,128)S(1)} %bitcast.22), channel_id=1, source_target_pairs={{1,0},{2,1},{3,2},{4,3},{5,4},{6,5},{7,6},{8,7},{9,8},{10,9},{11,1... | collective-permute-start | bytes 6152 | tf_op jit(solution)/shard_map/ppermute | solution.py:264
  16.7 0.0 collective-permute-done.2
  16.7 0.2 collective-permute-done.1
  16.9 1.1 %collective-permute-done = f32[4,128]{1,0:T(4,128)S(1)} collective-permute-done((f32[4,128]{1,0:T(4,128)S(1)}, f32[4,128]{1,0:T(4,128)S(1)}, u32[]{:S(2)}, u32[]{:S(2)}) %collective-permute-start) | collective-permute-done | bytes 2080 | tf_op jit(solution)/shard_map/ppermute | solution.py:264
  18.0 1.4 %collective-permute-start.5 = (f32[16,128]{1,0:T(8,128)S(1)}, f32[16,128]{1,0:T(8,128)S(1)}, u32[]{:S(2)}, u32[]{:S(2)}) collective-permute-start(f32[16,128]{1,0:T(8,128)S(1)} %pad_maximum_fusion), channel_id=1, source_target_pairs={{12,0},{13,1},{14,2},{15,3},{0,4},{1,5},{2,6},{3,7},{4,8},{5,9},{6... | collective-permute-start | bytes 24584 | tf_op jit(solution)/shard_map/ppermute | solution.py:264
  19.4 3.8 %collective-permute-start.4 = (f32[16,128]{1,0:T(8,128)S(1)}, f32[16,128]{1,0:T(8,128)S(1)}, u32[]{:S(2)}, u32[]{:S(2)}) collective-permute-start(f32[16,128]{1,0:T(8,128)S(1)} %pad_maximum_fusion), channel_id=1, source_target_pairs={{8,0},{9,1},{10,2},{11,3},{12,4},{13,5},{14,6},{15,7},{0,8},{1,9},... | collective-permute-start | bytes 24584 | tf_op jit(solution)/shard_map/ppermute | solution.py:264
  23.3 0.2 collective-permute-start.3
  23.5 0.7 %edges.1 = (f32[4,512]{1,0:T(4,128)S(1)}, f32[4,512]{1,0:T(4,128)S(1)}) custom-call(f32[4,512,128]{2,1,0:T(8,128)S(1)} %bitcast.12), custom_call_target="tpu_custom_call" | custom-call | bytes 33554432 | tf_op jit(solution)/shard_map/edges/pallas_call | solution.py:294
  24.2 0.0 collective-permute-done.5
  24.2 2.8 %collective-permute-done.4 = f32[16,128]{1,0:T(8,128)S(1)} collective-permute-done((f32[16,128]{1,0:T(8,128)S(1)}, f32[16,128]{1,0:T(8,128)S(1)}, u32[]{:S(2)}, u32[]{:S(2)}) %collective-permute-start.4) | collective-permute-done | bytes 8224 | tf_op jit(solution)/shard_map/ppermute | solution.py:264
  27.0 2.0 %collective-permute-done.3 = f32[16,128]{1,0:T(8,128)S(1)} collective-permute-done((f32[16,128]{1,0:T(8,128)S(1)}, f32[16,128]{1,0:T(8,128)S(1)}, u32[]{:S(2)}, u32[]{:S(2)}) %collective-permute-start.3) | collective-permute-done | bytes 8224 | tf_op jit(solution)/shard_map/ppermute | solution.py:264
  29.1 0.0 all-to-all-done.gathered_ref
  29.1 1.2 %source.1 = f32[16,136,128]{2,1,0:T(8,128)} custom-call(f32[16,136,128]{2,1,0:T(8,128)S(1)} %all-to-all-done.gathered_ref, f32[128,128]{1,0:T(8,128)S(1)} %maximum_bitcast_fusion.faces_ref), custom_call_target="tpu_custom_call" | custom-call | tf_op jit(solution)/shard_map/source/pallas_call | solution.py:309
  30.3 4.4 %all-to-all-start.1 = ((f32[16,136,128]{2,1,0:T(8,128)}), f32[16,136,128]{2,1,0:T(8,128)S(1)}, u32[]{:S(2)}, u32[]{:S(2)}) async-start(f32[16,136,128]{2,1,0:T(8,128)} %source.1), calls=%async_computation.1 | async-start | bytes 2228224 | tf_op jit(solution)/shard_map/all_to_all | solution.py:322
  34.7 0.0 copy-start.1
  34.7 0.0 copy-start.2
  34.7 0.0 collective-permute-start.6
  34.7 0.5 collective-permute-start.7
  35.2 0.9 %collective-permute-done.6.right_ref = f32[4,512]{1,0:T(4,128)S(1)} collective-permute-done((f32[4,512]{1,0:T(4,128)S(1)}, f32[4,512]{1,0:T(4,128)S(1)}, u32[]{:S(2)}, u32[]{:S(2)}) %collective-permute-start.6) | collective-permute-done | bytes 8224 | tf_op jit(solution)/shard_map/ppermute | solution.py:324
  36.1 1.7 %collective-permute-done.7.left_ref = f32[4,512]{1,0:T(4,128)S(1)} collective-permute-done((f32[4,512]{1,0:T(4,128)S(1)}, f32[4,512]{1,0:T(4,128)S(1)}, u32[]{:S(2)}, u32[]{:S(2)}) %collective-permute-start.7) | collective-permute-done | bytes 8224 | tf_op jit(solution)/shard_map/ppermute | solution.py:325
  37.8 4.0 %partial.1.partial_ref = f32[4,512,128]{2,1,0:T(8,128)S(1)} custom-call(f32[4,512,128]{2,1,0:T(8,128)S(1)} %bitcast.13, f32[4,512,128]{2,1,0:T(8,128)S(1)} %bitcast.14, f32[4,512,128]{2,1,0:T(8,128)S(1)} %bitcast.15, f32[4,512]{1,0:T(4,128)S(1)} %collective-permute-done.6.right_ref, f32[4,512]{1,0:T(4,128)S(1)} %collective-permute-done.7.left_ref), custom_call_target="tpu_custom_call" | custom-call | flops 26214400 | bytes 4194304 | tf_op jit(solution)/shard_map/partial/pallas_call | solution.py:332
  41.9 9.9 %all-to-all-done.1.packed_ref = f32[16,136,128]{2,1,0:T(8,128)S(1)} async-done(((f32[16,136,128]{2,1,0:T(8,128)}), f32[16,136,128]{2,1,0:T(8,128)S(1)}, u32[]{:S(2)}, u32[]{:S(2)}) %all-to-all-start.1) | async-done | bytes 1114144 | tf_op jit(solution)/shard_map/all_to_all | solution.py:322
  51.7 0.0 copy-done.1
  51.7 0.0 copy-done.2
  51.7 1.4 %finish.1 = (f32[4,512,128]{2,1,0:T(8,128)}, f32[4,512,128]{2,1,0:T(8,128)}) custom-call(f32[16,136,128]{2,1,0:T(8,128)S(1)} %all-to-all-done.1.packed_ref, f32[4,512,128]{2,1,0:T(8,128)S(1)} %partial.1.partial_ref, f32[4,512,128]{2,1,0:T(8,128)S(1)} %bitcast.16, s32[4,128]{1,0:T(4,128)S(1)} %bitcast.17, f32[4,128]{1,0:T(4,128)S(1)} %bitcast.18), custom_call_target="tpu_custom_call" | custom-call | tf_op jit(solution)/shard_map/finish/pallas_call | solution.py:353
  (4 shorter events, 0.1 us)
Async XLA Ops:
  2.7 8.4 %copy-start = (f32[1,4,512,128]{3,2,1,0:T(8,128)S(1)}, f32[1,4,512,128]{3,2,1,0:T(8,128)}, u32[]{:S(2)}) copy-start(f32[1,4,512,128]{3,2,1,0:T(8,128)} %param.4) | copy-start | bytes 3145732
  2.7 26.4 %all-to-all-start = ((f32[16,136,128]{2,1,0:T(8,128)}), f32[16,136,128]{2,1,0:T(8,128)S(1)}, u32[]{:S(2)}, u32[]{:S(2)}) async-start(f32[16,136,128]{2,1,0:T(8,128)} %send.1), calls=%async_computation | async-start | bytes 2228224 | tf_op jit(solution)/shard_map/all_to_all | solution.py:306
  11.1 5.6 %collective-permute-start.2 = (f32[4,128]{1,0:T(4,128)S(1)}, f32[4,128]{1,0:T(4,128)S(1)}, u32[]{:S(2)}, u32[]{:S(2)}) collective-permute-start(f32[4,128]{1,0:T(4,128)S(1)} %bitcast.20), channel_id=1, source_target_pairs={{3,0},{4,1},{5,2},{6,3},{7,4},{8,5},{9,6},{10,7},{11,8},{12,9},{13... | collective-permute-start | bytes 6152 | tf_op jit(solution)/shard_map/ppermute | solution.py:264
  11.2 5.7 %collective-permute-start.1 = (f32[4,128]{1,0:T(4,128)S(1)}, f32[4,128]{1,0:T(4,128)S(1)}, u32[]{:S(2)}, u32[]{:S(2)}) collective-permute-start(f32[4,128]{1,0:T(4,128)S(1)} %bitcast.21), channel_id=1, source_target_pairs={{2,0},{3,1},{4,2},{5,3},{6,4},{7,5},{8,6},{9,7},{10,8},{11,9},{12,... | collective-permute-start | bytes 6152 | tf_op jit(solution)/shard_map/ppermute | solution.py:264
  15.6 2.4 %collective-permute-start = (f32[4,128]{1,0:T(4,128)S(1)}, f32[4,128]{1,0:T(4,128)S(1)}, u32[]{:S(2)}, u32[]{:S(2)}) collective-permute-start(f32[4,128]{1,0:T(4,128)S(1)} %bitcast.22), channel_id=1, source_target_pairs={{1,0},{2,1},{3,2},{4,3},{5,4},{6,5},{7,6},{8,7},{9,8},{10,9},{11,1... | collective-permute-start | bytes 6152 | tf_op jit(solution)/shard_map/ppermute | solution.py:264
  18.0 6.2 %collective-permute-start.5 = (f32[16,128]{1,0:T(8,128)S(1)}, f32[16,128]{1,0:T(8,128)S(1)}, u32[]{:S(2)}, u32[]{:S(2)}) collective-permute-start(f32[16,128]{1,0:T(8,128)S(1)} %pad_maximum_fusion), channel_id=1, source_target_pairs={{12,0},{13,1},{14,2},{15,3},{0,4},{1,5},{2,6},{3,7},{4,8},{5,9},{6... | collective-permute-start | bytes 24584 | tf_op jit(solution)/shard_map/ppermute | solution.py:264
  19.4 7.6 %collective-permute-start.4 = (f32[16,128]{1,0:T(8,128)S(1)}, f32[16,128]{1,0:T(8,128)S(1)}, u32[]{:S(2)}, u32[]{:S(2)}) collective-permute-start(f32[16,128]{1,0:T(8,128)S(1)} %pad_maximum_fusion), channel_id=1, source_target_pairs={{8,0},{9,1},{10,2},{11,3},{12,4},{13,5},{14,6},{15,7},{0,8},{1,9},... | collective-permute-start | bytes 24584 | tf_op jit(solution)/shard_map/ppermute | solution.py:264
  23.3 5.8 %collective-permute-start.3 = (f32[16,128]{1,0:T(8,128)S(1)}, f32[16,128]{1,0:T(8,128)S(1)}, u32[]{:S(2)}, u32[]{:S(2)}) collective-permute-start(f32[16,128]{1,0:T(8,128)S(1)} %pad_maximum_fusion), channel_id=1, source_target_pairs={{4,0},{5,1},{6,2},{7,3},{8,4},{9,5},{10,6},{11,7},{12,8},{13,9},{1... | collective-permute-start | bytes 24584 | tf_op jit(solution)/shard_map/ppermute | solution.py:264
  30.3 21.4 %all-to-all-start.1 = ((f32[16,136,128]{2,1,0:T(8,128)}), f32[16,136,128]{2,1,0:T(8,128)S(1)}, u32[]{:S(2)}, u32[]{:S(2)}) async-start(f32[16,136,128]{2,1,0:T(8,128)} %source.1), calls=%async_computation.1 | async-start | bytes 2228224 | tf_op jit(solution)/shard_map/all_to_all | solution.py:322
  34.7 17.1 %copy-start.1 = (s32[4,1,128]{2,1,0:T(1,128)S(1)}, s32[4,1,128]{2,1,0:T(1,128)}, u32[]{:S(2)}) copy-start(s32[4,1,128]{2,1,0:T(1,128)} %param.5) | copy-start | bytes 6148
  34.7 17.1 %copy-start.2 = (f32[4,1,128]{2,1,0:T(1,128)S(1)}, f32[4,1,128]{2,1,0:T(1,128)}, u32[]{:S(2)}) copy-start(f32[4,1,128]{2,1,0:T(1,128)} %param.7) | copy-start | bytes 6148
  34.7 1.4 %collective-permute-start.6 = (f32[4,512]{1,0:T(4,128)S(1)}, f32[4,512]{1,0:T(4,128)S(1)}, u32[]{:S(2)}, u32[]{:S(2)}) collective-permute-start(f32[4,512]{1,0:T(4,128)S(1)} %get-tuple-element.16), channel_id=1, source_target_pairs={{1,0},{2,1},{3,2},{4,3},{5,4},{6,5},{7,6},{8,7},{9,8},{10,9},{11,1... | collective-permute-start | bytes 24584 | tf_op jit(solution)/shard_map/ppermute | solution.py:324
  34.7 3.1 %collective-permute-start.7 = (f32[4,512]{1,0:T(4,128)S(1)}, f32[4,512]{1,0:T(4,128)S(1)}, u32[]{:S(2)}, u32[]{:S(2)}) collective-permute-start(f32[4,512]{1,0:T(4,128)S(1)} %get-tuple-element.17), channel_id=1, source_target_pairs={{0,1},{1,2},{2,3},{3,4},{4,5},{5,6},{6,7},{7,8},{8,9},{9,10},{10,1... | collective-permute-start | bytes 24584 | tf_op jit(solution)/shard_map/ppermute | solution.py:325

commit v7 on v6

--- a/solution.py
+++ b/solution.py
@@ -243,14 +243,26 @@
                 return carry
 
             lax.fori_loop(0, depth // ROWS, strip, 0, unroll=True)
+            if 0 < j < per - 1:
+                for k, (src, dst) in enumerate(((res_ref, residual_ref), (next_ref, new_ref))):
+                    span = pl.ds(j * depth, depth)
+                    copy = pltpu.make_async_copy(
+                        src.at[c, span, :], dst.at[c, span, :], sems.at[2 * (c * per + j) + k]
+                    )
+                    copy.start()
+                    copies.append(copy)
         for first, extra in ((0, at_head), (axial - ROWS, at_tail)):
             out = res_ref[c, first : first + ROWS, :] + extra
             res_ref[c, first : first + ROWS, :] = out
             next_ref[c, first : first + ROWS, :] = cells_ref[c, first : first + ROWS, :] - PSEUDO_STEP * out
-        for k, (src, dst) in enumerate(((res_ref, residual_ref), (next_ref, new_ref))):
-            copy = pltpu.make_async_copy(src.at[c], dst.at[c], sems.at[2 * c + k])
-            copy.start()
-            copies.append(copy)
+        for j in (0, per - 1):
+            for k, (src, dst) in enumerate(((res_ref, residual_ref), (next_ref, new_ref))):
+                span = pl.ds(j * depth, depth)
+                copy = pltpu.make_async_copy(
+                    src.at[c, span, :], dst.at[c, span, :], sems.at[2 * (c * per + j) + k]
+                )
+                copy.start()
+                copies.append(copy)
     for copy in copies:
         copy.wait()
 
@@ -358,7 +370,7 @@
         scratch_shapes=[
             pltpu.VMEM(cells.shape, jnp.float32),
             pltpu.VMEM(cells.shape, jnp.float32),
-            pltpu.SemaphoreType.DMA((8,)),
+            pltpu.SemaphoreType.DMA((2 * inst_count,)),
         ],
         compiler_params=pltpu.CompilerParams(vmem_limit_bytes=16 << 20),
         name="finish",

time: 53.5 us -> 53.6 us (level)
  no operation moved by 1% of the time
where the time goes in v7:
time: 53.6 us; the launch traced here: 53.4 us
  starting transfers between devices  24.3 us (45%)
  waiting for transfers between devices  18.6 us (35%)
  Pallas kernels  9.6 us (18%)
  between operations  0.74 us (1%)
    ppermute x6, starting transfers between devices, collected(): blocks.append(lax.ppermute(block, axis, pairs))  11.1 us
    all_to_all x1, waiting for transfers between devices, on_device(): packed = lax.all_to_all(packed, 'inst', 0, 0, axis_index_groups=[COLLECT])  9.88 us
    all_to_all x1, starting transfers between devices, on_device(): gathered = lax.all_to_all(sent, 'inst', 0, 0, axis_index_groups=[SPREAD])  8.38 us
    ppermute x6, waiting for transfers between devices, collected(): blocks.append(lax.ppermute(block, axis, pairs))  6.13 us
    all_to_all x1, starting transfers between devices, on_device(): packed = lax.all_to_all(packed, 'inst', 0, 0, axis_index_groups=[COLLECT])  4.36 us
    pallas_call x1, Pallas kernels, on_device(): pl.pallas_call(partial_kernel, grid=(blocks,), out_shape=pltpu.VMEM(cells...  4.03 us
    pallas_call x1, Pallas kernels, on_device(): pl.pallas_call(send_kernel, out_shape=jax.ShapeDtypeStruct((inst_count, d...  2.06 us
    ppermute x1, waiting for transfers between devices, on_device(): lax.ppermute(tail, 'cell', [(i, (i + 1) % cell_count) for i in range(cell...  1.73 us
  transfers between devices with their start and end apart: 10, of which 7 were waited for; matrix products, arithmetic and copies ran while one was open for 0% of the time, Pallas kernels for 9%

profile of v7, /device:TPU:64, one launch (start us, length us, event | category | flops | bytes accessed | tf_op | source)
XLA Modules:
  0.0 53.4 jit_solution(1711071697715839799)
XLA Ops:
  0.6 2.1 %send.1 = f32[16,136,128]{2,1,0:T(8,128)} custom-call(f32[16,128,128]{2,1,0:T(8,128)} %bitcast.10, s32[4,1,128]{2,1,0:T(1,128)} %face_ref.1), custom_call_target="tpu_custom_call" | custom-call | tf_op jit(solution)/shard_map/send/pallas_call | solution.py:290
  2.7 0.0 copy-start
  2.7 8.4 %all-to-all-start = ((f32[16,136,128]{2,1,0:T(8,128)}), f32[16,136,128]{2,1,0:T(8,128)S(1)}, u32[]{:S(2)}, u32[]{:S(2)}) async-start(f32[16,136,128]{2,1,0:T(8,128)} %send.1), calls=%async_computation | async-start | bytes 2228224 | tf_op jit(solution)/shard_map/all_to_all | solution.py:318
  11.1 0.0 copy-done
  11.1 0.1 collective-permute-start.2
  11.2 4.4 %collective-permute-start.1 = (f32[4,128]{1,0:T(4,128)S(1)}, f32[4,128]{1,0:T(4,128)S(1)}, u32[]{:S(2)}, u32[]{:S(2)}) collective-permute-start(f32[4,128]{1,0:T(4,128)S(1)} %bitcast.21), channel_id=1, source_target_pairs={{2,0},{3,1},{4,2},{5,3},{6,4},{7,5},{8,6},{9,7},{10,8},{11,9},{12,... | collective-permute-start | bytes 6152 | tf_op jit(solution)/shard_map/ppermute | solution.py:276
  15.6 1.1 %collective-permute-start = (f32[4,128]{1,0:T(4,128)S(1)}, f32[4,128]{1,0:T(4,128)S(1)}, u32[]{:S(2)}, u32[]{:S(2)}) collective-permute-start(f32[4,128]{1,0:T(4,128)S(1)} %bitcast.22), channel_id=1, source_target_pairs={{1,0},{2,1},{3,2},{4,3},{5,4},{6,5},{7,6},{8,7},{9,8},{10,9},{11,1... | collective-permute-start | bytes 6152 | tf_op jit(solution)/shard_map/ppermute | solution.py:276
  16.7 0.0 collective-permute-done.2
  16.7 0.2 collective-permute-done.1
  16.9 1.1 %collective-permute-done = f32[4,128]{1,0:T(4,128)S(1)} collective-permute-done((f32[4,128]{1,0:T(4,128)S(1)}, f32[4,128]{1,0:T(4,128)S(1)}, u32[]{:S(2)}, u32[]{:S(2)}) %collective-permute-start) | collective-permute-done | bytes 2080 | tf_op jit(solution)/shard_map/ppermute | solution.py:276
  18.0 1.4 %collective-permute-start.5 = (f32[16,128]{1,0:T(8,128)S(1)}, f32[16,128]{1,0:T(8,128)S(1)}, u32[]{:S(2)}, u32[]{:S(2)}) collective-permute-start(f32[16,128]{1,0:T(8,128)S(1)} %pad_maximum_fusion), channel_id=1, source_target_pairs={{12,0},{13,1},{14,2},{15,3},{0,4},{1,5},{2,6},{3,7},{4,8},{5,9},{6... | collective-permute-start | bytes 24584 | tf_op jit(solution)/shard_map/ppermute | solution.py:276
  19.4 3.8 %collective-permute-start.4 = (f32[16,128]{1,0:T(8,128)S(1)}, f32[16,128]{1,0:T(8,128)S(1)}, u32[]{:S(2)}, u32[]{:S(2)}) collective-permute-start(f32[16,128]{1,0:T(8,128)S(1)} %pad_maximum_fusion), channel_id=1, source_target_pairs={{8,0},{9,1},{10,2},{11,3},{12,4},{13,5},{14,6},{15,7},{0,8},{1,9},... | collective-permute-start | bytes 24584 | tf_op jit(solution)/shard_map/ppermute | solution.py:276
  23.3 0.2 collective-permute-start.3
  23.5 0.7 %edges.1 = (f32[4,512]{1,0:T(4,128)S(1)}, f32[4,512]{1,0:T(4,128)S(1)}) custom-call(f32[4,512,128]{2,1,0:T(8,128)S(1)} %bitcast.12), custom_call_target="tpu_custom_call" | custom-call | bytes 33554432 | tf_op jit(solution)/shard_map/edges/pallas_call | solution.py:306
  24.2 0.0 collective-permute-done.5
  24.2 2.8 %collective-permute-done.4 = f32[16,128]{1,0:T(8,128)S(1)} collective-permute-done((f32[16,128]{1,0:T(8,128)S(1)}, f32[16,128]{1,0:T(8,128)S(1)}, u32[]{:S(2)}, u32[]{:S(2)}) %collective-permute-start.4) | collective-permute-done | bytes 8224 | tf_op jit(solution)/shard_map/ppermute | solution.py:276
  27.0 2.0 %collective-permute-done.3 = f32[16,128]{1,0:T(8,128)S(1)} collective-permute-done((f32[16,128]{1,0:T(8,128)S(1)}, f32[16,128]{1,0:T(8,128)S(1)}, u32[]{:S(2)}, u32[]{:S(2)}) %collective-permute-start.3) | collective-permute-done | bytes 8224 | tf_op jit(solution)/shard_map/ppermute | solution.py:276
  29.1 0.0 all-to-all-done.gathered_ref
  29.1 1.2 %source.1 = f32[16,136,128]{2,1,0:T(8,128)} custom-call(f32[16,136,128]{2,1,0:T(8,128)S(1)} %all-to-all-done.gathered_ref, f32[128,128]{1,0:T(8,128)S(1)} %maximum_bitcast_fusion.faces_ref), custom_call_target="tpu_custom_call" | custom-call | tf_op jit(solution)/shard_map/source/pallas_call | solution.py:321
  30.3 4.4 %all-to-all-start.1 = ((f32[16,136,128]{2,1,0:T(8,128)}), f32[16,136,128]{2,1,0:T(8,128)S(1)}, u32[]{:S(2)}, u32[]{:S(2)}) async-start(f32[16,136,128]{2,1,0:T(8,128)} %source.1), calls=%async_computation.1 | async-start | bytes 2228224 | tf_op jit(solution)/shard_map/all_to_all | solution.py:334
  34.7 0.0 copy-start.1
  34.7 0.0 copy-start.2
  34.7 0.0 collective-permute-start.6
  34.7 0.5 collective-permute-start.7
  35.2 0.9 %collective-permute-done.6.right_ref = f32[4,512]{1,0:T(4,128)S(1)} collective-permute-done((f32[4,512]{1,0:T(4,128)S(1)}, f32[4,512]{1,0:T(4,128)S(1)}, u32[]{:S(2)}, u32[]{:S(2)}) %collective-permute-start.6) | collective-permute-done | bytes 8224 | tf_op jit(solution)/shard_map/ppermute | solution.py:336
  36.1 1.7 %collective-permute-done.7.left_ref = f32[4,512]{1,0:T(4,128)S(1)} collective-permute-done((f32[4,512]{1,0:T(4,128)S(1)}, f32[4,512]{1,0:T(4,128)S(1)}, u32[]{:S(2)}, u32[]{:S(2)}) %collective-permute-start.7) | collective-permute-done | bytes 8224 | tf_op jit(solution)/shard_map/ppermute | solution.py:337
  37.8 4.0 %partial.1.partial_ref = f32[4,512,128]{2,1,0:T(8,128)S(1)} custom-call(f32[4,512,128]{2,1,0:T(8,128)S(1)} %bitcast.13, f32[4,512,128]{2,1,0:T(8,128)S(1)} %bitcast.14, f32[4,512,128]{2,1,0:T(8,128)S(1)} %bitcast.15, f32[4,512]{1,0:T(4,128)S(1)} %collective-permute-done.6.right_ref, f32[4,512]{1,0:T(4,128)S(1)} %collective-permute-done.7.left_ref), custom_call_target="tpu_custom_call" | custom-call | flops 26214400 | bytes 4194304 | tf_op jit(solution)/shard_map/partial/pallas_call | solution.py:344
  41.9 9.9 %all-to-all-done.1.packed_ref = f32[16,136,128]{2,1,0:T(8,128)S(1)} async-done(((f32[16,136,128]{2,1,0:T(8,128)}), f32[16,136,128]{2,1,0:T(8,128)S(1)}, u32[]{:S(2)}, u32[]{:S(2)}) %all-to-all-start.1) | async-done | bytes 1114144 | tf_op jit(solution)/shard_map/all_to_all | solution.py:334
  51.7 0.0 copy-done.1
  51.7 0.0 copy-done.2
  51.7 1.6 %finish.1 = (f32[4,512,128]{2,1,0:T(8,128)}, f32[4,512,128]{2,1,0:T(8,128)}) custom-call(f32[16,136,128]{2,1,0:T(8,128)S(1)} %all-to-all-done.1.packed_ref, f32[4,512,128]{2,1,0:T(8,128)S(1)} %partial.1.partial_ref, f32[4,512,128]{2,1,0:T(8,128)S(1)} %bitcast.16, s32[4,128]{1,0:T(4,128)S(1)} %bitcast.17, f32[4,128]{1,0:T(4,128)S(1)} %bitcast.18), custom_call_target="tpu_custom_call" | custom-call | tf_op jit(solution)/shard_map/finish/pallas_call | solution.py:365
  (4 shorter events, 0.1 us)
Async XLA Ops:
  2.7 8.4 %copy-start = (f32[1,4,512,128]{3,2,1,0:T(8,128)S(1)}, f32[1,4,512,128]{3,2,1,0:T(8,128)}, u32[]{:S(2)}) copy-start(f32[1,4,512,128]{3,2,1,0:T(8,128)} %param.4) | copy-start | bytes 3145732
  2.7 26.4 %all-to-all-start = ((f32[16,136,128]{2,1,0:T(8,128)}), f32[16,136,128]{2,1,0:T(8,128)S(1)}, u32[]{:S(2)}, u32[]{:S(2)}) async-start(f32[16,136,128]{2,1,0:T(8,128)} %send.1), calls=%async_computation | async-start | bytes 2228224 | tf_op jit(solution)/shard_map/all_to_all | solution.py:318
  11.1 5.6 %collective-permute-start.2 = (f32[4,128]{1,0:T(4,128)S(1)}, f32[4,128]{1,0:T(4,128)S(1)}, u32[]{:S(2)}, u32[]{:S(2)}) collective-permute-start(f32[4,128]{1,0:T(4,128)S(1)} %bitcast.20), channel_id=1, source_target_pairs={{3,0},{4,1},{5,2},{6,3},{7,4},{8,5},{9,6},{10,7},{11,8},{12,9},{13... | collective-permute-start | bytes 6152 | tf_op jit(solution)/shard_map/ppermute | solution.py:276
  11.2 5.7 %collective-permute-start.1 = (f32[4,128]{1,0:T(4,128)S(1)}, f32[4,128]{1,0:T(4,128)S(1)}, u32[]{:S(2)}, u32[]{:S(2)}) collective-permute-start(f32[4,128]{1,0:T(4,128)S(1)} %bitcast.21), channel_id=1, source_target_pairs={{2,0},{3,1},{4,2},{5,3},{6,4},{7,5},{8,6},{9,7},{10,8},{11,9},{12,... | collective-permute-start | bytes 6152 | tf_op jit(solution)/shard_map/ppermute | solution.py:276
  15.6 2.4 %collective-permute-start = (f32[4,128]{1,0:T(4,128)S(1)}, f32[4,128]{1,0:T(4,128)S(1)}, u32[]{:S(2)}, u32[]{:S(2)}) collective-permute-start(f32[4,128]{1,0:T(4,128)S(1)} %bitcast.22), channel_id=1, source_target_pairs={{1,0},{2,1},{3,2},{4,3},{5,4},{6,5},{7,6},{8,7},{9,8},{10,9},{11,1... | collective-permute-start | bytes 6152 | tf_op jit(solution)/shard_map/ppermute | solution.py:276
  18.0 6.2 %collective-permute-start.5 = (f32[16,128]{1,0:T(8,128)S(1)}, f32[16,128]{1,0:T(8,128)S(1)}, u32[]{:S(2)}, u32[]{:S(2)}) collective-permute-start(f32[16,128]{1,0:T(8,128)S(1)} %pad_maximum_fusion), channel_id=1, source_target_pairs={{12,0},{13,1},{14,2},{15,3},{0,4},{1,5},{2,6},{3,7},{4,8},{5,9},{6... | collective-permute-start | bytes 24584 | tf_op jit(solution)/shard_map/ppermute | solution.py:276
  19.4 7.6 %collective-permute-start.4 = (f32[16,128]{1,0:T(8,128)S(1)}, f32[16,128]{1,0:T(8,128)S(1)}, u32[]{:S(2)}, u32[]{:S(2)}) collective-permute-start(f32[16,128]{1,0:T(8,128)S(1)} %pad_maximum_fusion), channel_id=1, source_target_pairs={{8,0},{9,1},{10,2},{11,3},{12,4},{13,5},{14,6},{15,7},{0,8},{1,9},... | collective-permute-start | bytes 24584 | tf_op jit(solution)/shard_map/ppermute | solution.py:276
  23.3 5.8 %collective-permute-start.3 = (f32[16,128]{1,0:T(8,128)S(1)}, f32[16,128]{1,0:T(8,128)S(1)}, u32[]{:S(2)}, u32[]{:S(2)}) collective-permute-start(f32[16,128]{1,0:T(8,128)S(1)} %pad_maximum_fusion), channel_id=1, source_target_pairs={{4,0},{5,1},{6,2},{7,3},{8,4},{9,5},{10,6},{11,7},{12,8},{13,9},{1... | collective-permute-start | bytes 24584 | tf_op jit(solution)/shard_map/ppermute | solution.py:276
  30.3 21.4 %all-to-all-start.1 = ((f32[16,136,128]{2,1,0:T(8,128)}), f32[16,136,128]{2,1,0:T(8,128)S(1)}, u32[]{:S(2)}, u32[]{:S(2)}) async-start(f32[16,136,128]{2,1,0:T(8,128)} %source.1), calls=%async_computation.1 | async-start | bytes 2228224 | tf_op jit(solution)/shard_map/all_to_all | solution.py:334
  34.7 17.1 %copy-start.1 = (s32[4,1,128]{2,1,0:T(1,128)S(1)}, s32[4,1,128]{2,1,0:T(1,128)}, u32[]{:S(2)}) copy-start(s32[4,1,128]{2,1,0:T(1,128)} %param.5) | copy-start | bytes 6148
  34.7 17.1 %copy-start.2 = (f32[4,1,128]{2,1,0:T(1,128)S(1)}, f32[4,1,128]{2,1,0:T(1,128)}, u32[]{:S(2)}) copy-start(f32[4,1,128]{2,1,0:T(1,128)} %param.7) | copy-start | bytes 6148
  34.7 1.4 %collective-permute-start.6 = (f32[4,512]{1,0:T(4,128)S(1)}, f32[4,512]{1,0:T(4,128)S(1)}, u32[]{:S(2)}, u32[]{:S(2)}) collective-permute-start(f32[4,512]{1,0:T(4,128)S(1)} %get-tuple-element.16), channel_id=1, source_target_pairs={{1,0},{2,1},{3,2},{4,3},{5,4},{6,5},{7,6},{8,7},{9,8},{10,9},{11,1... | collective-permute-start | bytes 24584 | tf_op jit(solution)/shard_map/ppermute | solution.py:336
  34.7 3.1 %collective-permute-start.7 = (f32[4,512]{1,0:T(4,128)S(1)}, f32[4,512]{1,0:T(4,128)S(1)}, u32[]{:S(2)}, u32[]{:S(2)}) collective-permute-start(f32[4,512]{1,0:T(4,128)S(1)} %get-tuple-element.17), channel_id=1, source_target_pairs={{0,1},{1,2},{2,3},{3,4},{4,5},{5,6},{6,7},{7,8},{8,9},{9,10},{10,1... | collective-permute-start | bytes 24584 | tf_op jit(solution)/shard_map/ppermute | solution.py:337
